TPU v7x, 128 devices: a whole 4x4x4 slice. The times are simulated.
128 devices in a mesh: slab: 64 (over z, x, y), sub: 2 (over core).
Axes of the slice: x: 4, y: 4, z: 4, core: 2. Of those that a mesh axis runs over, the one named last changes fastest.
Arguments:
- right_side: float32 [1024, 8, 128], P('slab'), may hold values from -7.2 to 7.2
- diagonal: float32 [1024, 128], P('slab'), may hold values from 0.02 to 2
- dense_blocks: float32 [1024, 128, 128], P(('slab', 'sub')), may hold values from -0.01171875 to 0.01171875
- tiles: float32 [1024, 8, 128, 128], P('slab', 'sub'), may hold values from -0.005859375 to 0.005859375
- tile_cols: int32 [1024, 8], P('slab', 'sub'), may hold values from 1 to 1023, as said below
- tile_counts: int32 [1024], P('slab'), may hold values from 0 to 8, as said below
Outputs:
- solution_field: float32 [1024, 8, 128], P('slab')
- residual: float32 [1024, 8, 128], P('slab')
Inputs may be any that keep to these rules, and one draw needn't show every extreme that they name: `tile_cols`: every slot of block row r below 1023 holds a column c with r < c <= min(r + 16, 1023); in the last block row c = r; the first block row holds column 1. Slots k < tile_counts[r] are live; the first block row has all of them live, the last none.
All inputs are finite; a program needn't handle non-finite values.
Results may differ from a plain program's by a relative error of at most 0.0003.
Values sent between devices are 32-bit elements; how exact they have to be, the bound alone decides.
A program may use at most 64 MiB of HBM per device.

v0:
```python
import jax
import jax.numpy as jnp
from jax import lax
from jax.sharding import PartitionSpec as P

ITERS = 4


def from_behind(array, axis, by):
    size = lax.axis_size(axis)
    pairs = [(i, i + by) for i in range(size) if 0 <= i + by < size]
    return lax.ppermute(array, axis, pairs)


def inner(first, second):
    return jnp.sum(first * second, axis=(0, 2))


def squares(residual):
    return lax.psum(inner(residual, residual), "slab")


def body(right_side, diagonal, dense_blocks, tiles, tile_cols, tile_counts):
    rows_dev = right_side.shape[0]
    nrhs = right_side.shape[1]
    width = right_side.shape[2]
    slots = tiles.shape[1]
    slab_pos = lax.axis_index("slab")
    core_pos = lax.axis_index("sub")
    first_row = slab_pos * rows_dev
    slot_ids = core_pos * slots + jnp.arange(slots, dtype=jnp.int32)
    live = (slot_ids[None, :] < tile_counts[:, None]).astype(jnp.float32)
    sigma = jnp.sqrt(jnp.sum(tiles * tiles, axis=(2, 3))) * live
    sigma_rows = jnp.sum(sigma, axis=1)
    dense_rows = dense_blocks.shape[0]
    dense_start = core_pos * dense_rows
    dense_sigma = jnp.sqrt(jnp.sum(dense_blocks * dense_blocks, axis=(1, 2)))
    spread_index = tile_cols.reshape(-1) - first_row
    span = 2 * rows_dev
    onehot = (spread_index[:, None] == jnp.arange(span, dtype=jnp.int32)[None, :]).astype(
        jnp.float32
    )
    solution_field = jnp.zeros_like(right_side)
    residual = right_side
    direction = right_side
    norm_now = squares(residual)
    for step in range(ITERS):
        following = from_behind(direction, "slab", -1)
        whole = jnp.concatenate([direction, following], axis=0)
        partner = jnp.take(whole, spread_index, axis=0).reshape(rows_dev, slots, nrhs, width)
        partner = partner * live[:, :, None, None]
        forward = jnp.einsum("ikab,iksb->isa", tiles, partner, precision=lax.Precision.HIGHEST)
        forward = forward + sigma_rows[:, None, None] * direction
        back = (
            jnp.einsum("ikab,isa->iksb", tiles, direction, precision=lax.Precision.HIGHEST)
            * live[:, :, None, None]
        )
        back = back + sigma[:, :, None, None] * partner
        back_flat = back.reshape(rows_dev * slots, nrhs * width)
        spread_all = jnp.dot(
            onehot.T, back_flat, precision=lax.Precision.HIGHEST, preferred_element_type=jnp.float32
        ).reshape(span, nrhs, width)
        arrived = from_behind(spread_all[rows_dev:], "slab", 1)
        returned = spread_all[:rows_dev] + arrived
        own_rows = lax.dynamic_slice_in_dim(direction, dense_start, dense_rows, 0)
        dense_out = dense_sigma[:, None, None] * own_rows + 0.5 * (
            jnp.einsum("bij,bsj->bsi", dense_blocks, own_rows, precision=lax.Precision.HIGHEST)
            + jnp.einsum("bji,bsj->bsi", dense_blocks, own_rows, precision=lax.Precision.HIGHEST)
        )
        dense_full = lax.dynamic_update_slice_in_dim(
            jnp.zeros_like(direction), dense_out, dense_start, 0
        )
        partial_image = forward + returned + dense_full
        image = lax.psum(partial_image, "sub") + diagonal[:, None, :] * direction
        alpha = norm_now / lax.psum(inner(direction, image), "slab")
        solution_field = solution_field + alpha[None, :, None] * direction
        residual = residual - alpha[None, :, None] * image
        norm_next = squares(residual)
        direction = residual + (norm_next / norm_now)[None, :, None] * direction
        norm_now = norm_next
    return (solution_field, residual)


def solution(mesh):
    return jax.shard_map(
        body,
        mesh=mesh,
        in_specs=(
            P("slab", None, None),
            P("slab", None),
            P(("slab", "sub"), None, None),
            P("slab", "sub", None, None),
            P("slab", "sub"),
            P("slab"),
        ),
        out_specs=(P("slab", None, None), P("slab", None, None)),
        check_vma=False,
    )
```

profile of v0, /device:TPU:0, one launch (start us, length us, event | category | flops | bytes accessed | tf_op | source)
XLA Modules:
  0.0 1431.0 jit_solution(235163221350871599)
XLA Ops:
  7.2 1.4 collective-permute-start
  9.6 2.6 multiply_reduce_fusion
  12.5 0.9 fusion.71
  14.5 4.0 fusion.7
  18.9 4.2 collective-permute-start.1
  23.3 1.7 collective-permute-done.1
  25.0 3.6 fusion.40
  29.9 30.3 %all-reduce.6.cloned.1.call-done = f32[16,8,128]{2,1,0:T(8,128)} async-done(((f32[16,8,128]{2,1,0:T(8,128)}), f32[16,8,128]{2,1,0:T(8,128)}) %all-reduce.6.cloned.1.call-update) | async-done | bytes 65552 | tf_op jit(solution)/shard_map/psum | solution.py:74
  60.2 1.0 multiply_reduce_fusion.8
  61.2 179.1 %all-reduce = (f32[8]{0:T(128)S(1)}, f32[8]{0:T(128)S(1)}) all-reduce(f32[8]{0:T(128)S(1)} %get-tuple-element.4, f32[8]{0:T(128)S(1)} %get-tuple-element.3), channel_id=1, replica_groups=mesh['slab'=64,'sub'=2] {'slab'}, use_global_device_ids=true, to_apply=%region_1.0 | all-reduce | flops 16 | bytes 128 | tf_op jit(solution)/shard_map/psum | solution.py:20
  240.3 1.0 multiply_reduce_fusion.7
  241.4 171.8 %psum.87 = f32[8]{0:T(128)S(1)} all-reduce(f32[8]{0:T(128)S(1)} %multiply_reduce_fusion.7), channel_id=1, replica_groups=mesh['slab'=64,'sub'=2] {'slab'}, use_global_device_ids=true, to_apply=%region_9.11 | all-reduce | flops 8 | bytes 64 | tf_op jit(solution)/shard_map/psum | solution.py:20
  413.1 0.9 multiply_add_fusion.6
  414.1 1.3 collective-permute-start.2
  415.4 4.9 collective-permute-done.2
  421.0 4.0 fusion.5
  425.4 4.0 collective-permute-start.3
  429.4 0.9 fusion.66
  430.4 0.7 collective-permute-done.3
  431.1 3.6 fusion.43
  436.0 19.0 %all-reduce.8.cloned.1.call-done = f32[16,8,128]{2,1,0:T(8,128)} async-done(((f32[16,8,128]{2,1,0:T(8,128)}), f32[16,8,128]{2,1,0:T(8,128)}) %all-reduce.8.cloned.1.call-update) | async-done | bytes 65552 | tf_op jit(solution)/shard_map/psum | solution.py:74
  455.0 1.0 multiply_reduce_fusion.6
  456.0 179.1 %psum.89 = f32[8]{0:T(128)S(1)} all-reduce(f32[8]{0:T(128)S(1)} %multiply_reduce_fusion.6), channel_id=1, replica_groups=mesh['slab'=64,'sub'=2] {'slab'}, use_global_device_ids=true, to_apply=%region_12.14 | all-reduce | flops 8 | bytes 64 | tf_op jit(solution)/shard_map/psum | solution.py:75
  635.1 1.0 multiply_reduce_fusion.5
  636.1 171.8 %psum.90 = f32[8]{0:T(128)S(1)} all-reduce(f32[8]{0:T(128)S(1)} %get-tuple-element.9), channel_id=1, replica_groups=mesh['slab'=64,'sub'=2] {'slab'}, use_global_device_ids=true, to_apply=%region_14.16 | all-reduce | flops 8 | bytes 64 | tf_op jit(solution)/shard_map/psum | solution.py:20
  808.0 1.3 collective-permute-start.4
  809.3 4.9 collective-permute-done.4
  814.9 4.0 fusion.3
  819.3 3.8 collective-permute-start.5
  823.1 0.9 fusion.61
  824.1 0.9 collective-permute-done.5
  825.0 3.6 fusion.46
  829.9 19.0 %all-reduce.10.cloned.1.call-done = f32[16,8,128]{2,1,0:T(8,128)} async-done(((f32[16,8,128]{2,1,0:T(8,128)}), f32[16,8,128]{2,1,0:T(8,128)}) %all-reduce.10.cloned.1.call-update) | async-done | bytes 65552 | tf_op jit(solution)/shard_map/psum | solution.py:74
  848.9 1.0 multiply_reduce_fusion.4
  849.9 179.1 %psum.92 = f32[8]{0:T(128)S(1)} all-reduce(f32[8]{0:T(128)S(1)} %multiply_reduce_fusion.4), channel_id=1, replica_groups=mesh['slab'=64,'sub'=2] {'slab'}, use_global_device_ids=true, to_apply=%region_17.19 | all-reduce | flops 8 | bytes 64 | tf_op jit(solution)/shard_map/psum | solution.py:75
  1029.0 1.0 multiply_reduce_fusion.3
  1030.0 171.8 %psum.93 = f32[8]{0:T(128)S(1)} all-reduce(f32[8]{0:T(128)S(1)} %get-tuple-element.7), channel_id=1, replica_groups=mesh['slab'=64,'sub'=2] {'slab'}, use_global_device_ids=true, to_apply=%region_19.21 | all-reduce | flops 8 | bytes 64 | tf_op jit(solution)/shard_map/psum | solution.py:20
  1201.9 1.3 collective-permute-start.6
  1203.2 4.9 collective-permute-done.6
  1208.8 4.0 fusion.1
  1213.2 4.1 collective-permute-start.7
  1217.2 0.9 fusion.56
  1218.2 0.7 collective-permute-done.7
  1218.9 3.6 fusion.49
  1223.7 19.1 %all-reduce.12.cloned.1.call-done = f32[16,8,128]{2,1,0:T(8,128)} async-done(((f32[16,8,128]{2,1,0:T(8,128)}), f32[16,8,128]{2,1,0:T(8,128)}) %all-reduce.12.cloned.1.call-update) | async-done | bytes 65552 | tf_op jit(solution)/shard_map/psum | solution.py:74
  1242.8 1.0 multiply_reduce_fusion.2
  1243.7 179.1 %psum.95 = f32[8]{0:T(128)S(1)} all-reduce(f32[8]{0:T(128)S(1)} %multiply_reduce_fusion.2), channel_id=1, replica_groups=mesh['slab'=64,'sub'=2] {'slab'}, use_global_device_ids=true, to_apply=%region_22.24 | all-reduce | flops 8 | bytes 64 | tf_op jit(solution)/shard_map/psum | solution.py:75
  1422.8 1.6 multiply_subtract_fusion
  (91 shorter events, 11.5 us)
Async XLA Ops:
  7.2 5.3 copy-start.5
  7.2 5.0 copy-start.12
  7.2 5.3 copy-start.4
  7.2 53.0 %all-reduce.6.cloned.1.call-start = ((), (), s32[]{:S(2)}) async-start(), calls=%async_computation | async-start | bytes 131072 | tf_op jit(solution)/shard_map/psum | solution.py:74
  7.2 6.5 collective-permute-start
  14.4 10.6 copy-start
  18.5 41.7 %copy-start.7 = (f32[16,128]{1,0:T(8,128)S(1)}, f32[16,128]{1,0:T(8,128)}, u32[]{:S(2)}) copy-start(f32[16,128]{1,0:T(8,128)} %param.9) | copy-start | bytes 24580
  18.9 6.1 collective-permute-start.1
  29.2 0.6 copy-start.9
  29.8 425.2 %all-reduce.8.cloned.1.call-start = ((), (), s32[]{:S(2)}) async-start(), calls=%async_computation.1 | async-start | bytes 131072 | tf_op jit(solution)/shard_map/psum | solution.py:74
  414.1 6.2 collective-permute-start.2
  420.9 10.3 copy-start.1
  425.0 210.1 %copy-start.6 = (f32[16,8,128]{2,1,0:T(8,128)S(1)}, f32[16,8,128]{2,1,0:T(8,128)}, u32[]{:S(2)}) copy-start(f32[16,8,128]{2,1,0:T(8,128)} %all-reduce.6.cloned.1.call-done) | copy-start | bytes 196612
  425.4 5.7 collective-permute-start.3
  435.3 0.6 copy-start.10
  435.9 413.0 %all-reduce.10.cloned.1.call-start = ((), (), s32[]{:S(2)}) async-start(), calls=%async_computation.2 | async-start | bytes 131072 | tf_op jit(solution)/shard_map/psum | solution.py:74
  808.0 6.1 collective-permute-start.4
  814.8 10.3 copy-start.2
  819.3 5.7 collective-permute-start.5
  829.1 0.6 copy-start.11
  829.8 413.0 %all-reduce.12.cloned.1.call-start = ((), (), s32[]{:S(2)}) async-start(), calls=%async_computation.3 | async-start | bytes 131072 | tf_op jit(solution)/shard_map/psum | solution.py:74
  1201.9 6.1 collective-permute-start.6
  1208.7 10.3 copy-start.3
  1213.2 5.7 collective-permute-start.7
  1223.0 0.6 copy-start.8
Sparse Core Ops, SparseCore 0:
  29.9 30.2 all-reduce.5
  436.0 18.9 all-reduce.7
  829.9 18.9 all-reduce.9
  1223.8 18.9 all-reduce.11
where the time goes:
time: 1430 us
  blocking collectives  1230 us (86%)
  waiting for transfers between devices  107 us (7%)
  matrix products  37.3 us (3%)
  starting transfers between devices  21.6 us (2%)
  between operations  14.3 us (1%)
    psum x4, blocking collectives, squares(): return lax.psum(inner(residual, residual), 'slab')  694 us
    psum x3, blocking collectives, body(): alpha = norm_now / lax.psum(inner(direction, image), 'slab')  537 us
    psum x4, waiting for transfers between devices, body(): image = lax.psum(partial_image, 'sub') + diagonal[:, None, :] * direction  87.5 us
  transfers between devices with their start and end apart: 12, of which 12 were waited for; matrix products, arithmetic and copies ran while one was open for 1% of the time, Pallas kernels for 0%

commit v1 on v0

v1 whole, which is shorter than its diff:
```python
import functools
import jax
import jax.numpy as jnp
from jax import lax
from jax.experimental import pallas as pl
from jax.experimental.pallas import tpu as pltpu
from jax.sharding import PartitionSpec as P

MESH = pl.DeviceIdType.MESH
F32 = jnp.float32
BF16 = jnp.bfloat16
ITERS = 4
ROWS = 16
SLOTS = 4
NRHS = 8
W = 128
SLABS = 64


def split(x):
    hi = x.astype(BF16)
    return hi, (x - hi.astype(F32)).astype(BF16)


def axis_peer(s, axis, d):
    z, x, y = s // 16, (s // 4) % 4, s % 4
    if axis == 0:
        y = (y + d) % 4
    if axis == 1:
        x = (x + d) % 4
    if axis == 2:
        z = (z + d) % 4
    return z * 16 + x * 4 + y


def kernel(cols, counts, b_ref, diag_ref, dense_hbm, tiles_hbm, x_ref, r_ref,
           tf, df, wt, dw, gm, sq, sig, krylov, halo, qout, qin, pout, pin, dg, snout, snin, vs, bst,
           thout, thin, arout, arin, tile_sem, dense_sem, peer_ss, peer_rs, halo_ss, halo_rs, q_ss, q_rs, sn_ss, sn_rs, th_ss, th_rs, ar_ss, ar_rs):
    s = lax.axis_index("slab")
    c = lax.axis_index("sub")
    after = ((s + 1) % SLABS, c)
    before = ((s + SLABS - 1) % SLABS, c)
    peer = (s, 1 - c)
    first = s * ROWS

    tile_copies = [pltpu.make_async_copy(tiles_hbm.at[pl.ds(4 * i, 4)], tf.at[pl.ds(4 * i, 4)], tile_sem.at[i]) for i in range(4)]
    dense_copy = pltpu.make_async_copy(dense_hbm, df, dense_sem)
    for cp in tile_copies:
        cp.start()
    dense_copy.start()

    barrier = pltpu.get_barrier_semaphore()
    axes = [(a, d) for a in range(3) for d in (1, 2, 3)]
    for dev in [after, before, peer] + [(axis_peer(s, a, d), c) for a, d in axes]:
        pl.semaphore_signal(barrier, inc=1, device_id=dev, device_id_type=MESH)

    def remote(src, dst, ss, rs, dev):
        return pltpu.make_async_remote_copy(src_ref=src, dst_ref=dst, send_sem=ss, recv_sem=rs, device_id=dev, device_id_type=MESH)

    lane = lax.broadcasted_iota(jnp.int32, (8, W), 1)
    col_lanes = []
    for g in range(4):
        cv = jnp.zeros((8, W), jnp.int32)
        for u in range(16):
            t = g * 16 + u
            cv = jnp.where(lane // 8 == u, cols[t // SLOTS, t % SLOTS] - first, cv)
        col_lanes.append(cv)
    cv = jnp.concatenate(col_lanes, axis=1)
    sub_of = lax.broadcasted_iota(jnp.int32, (8, 512), 0)
    lane_of = lax.broadcasted_iota(jnp.int32, (8, 512), 1)
    same = lane_of % 8 == sub_of
    for j in range(0, 2 * ROWS, 2):
        top = jnp.where((cv == j) & same, 1.0, 0.0)
        low = jnp.where((cv == j + 1) & same, 1.0, 0.0)
        gm[8 * j:8 * j + 16, :] = jnp.concatenate([top, low], axis=0).astype(BF16)

    for i in range(4):
        tile_copies[i].wait()

        def prep(rr, carry):
            r = 4 * i + rr
            for k in range(SLOTS):
                live = jnp.where(c * SLOTS + k < counts[r], 1.0, 0.0).astype(F32)
                t = tf[r, k] * live
                hi, lo = split(t)
                wt[r, 0:W, W * k:W * k + W] = hi
                wt[r, W:2 * W, W * k:W * k + W] = lo
                sq[r * SLOTS + k] = jnp.sum((t * t).reshape(16, 8, W), axis=0)
            return carry

        lax.fori_loop(0, 4, prep, 0)
    total = jnp.sum(jnp.sum(sq[...], axis=2, keepdims=True), axis=1, keepdims=True)
    sigma = jnp.broadcast_to(jnp.sqrt(total), (64, 8, W))
    sig[...] = sigma
    sigma2 = sigma.reshape(512, W)
    s_hi = sigma2.astype(BF16)
    rest = sigma2 - s_hi.astype(F32)
    s_mid = rest.astype(BF16)
    s_lo = (rest - s_mid.astype(F32)).astype(BF16)
    scol = jnp.dot(gm[...], jnp.concatenate([s_hi, s_mid], axis=1), preferred_element_type=F32)
    scol = scol[:, :W] + scol[:, W:] + jnp.dot(gm[...], s_lo, preferred_element_type=F32)
    scol = scol.reshape(2 * ROWS, NRHS, W)
    snout[...] = scol[ROWS:]

    dense_copy.wait()
    dsum = jnp.zeros((8, W), F32)
    dsig = []
    for j in range(8):
        d = df[j]
        sqd = jnp.sum((d * d).reshape(16, 8, W), axis=0)
        dtot = jnp.sum(jnp.sum(sqd, axis=1, keepdims=True), axis=0, keepdims=True)
        ds = jnp.broadcast_to(jnp.sqrt(dtot), (8, W))
        dsig.append(ds)
        dsum = dsum + ds
        hi, lo = split(0.5 * (d + d.T))
        dw[j, :, 0:W] = hi
        dw[j, :, W:2 * W] = lo
    srow = jnp.sum(sig[...].reshape(ROWS, SLOTS, 8, W), axis=1)
    half = 0.5 * diag_ref[...]
    dg[...] = srow + scol[:ROWS] + half[:, None, :]
    for j in range(8):
        dg[8 * c + j] = dg[8 * c + j] + dsig[j]
    diag_sum = jnp.sum(half, axis=0, keepdims=True)
    diag_sum = jnp.sum(diag_sum, axis=1, keepdims=True)
    thout[0] = (2.0 * jnp.sum(sig[...], axis=0) + dsum) * W + diag_sum

    pl.semaphore_wait(barrier, 12)

    sn_copy = remote(snout, snin, sn_ss, sn_rs, after)
    theta_peer = remote(thout.at[0], thin.at[0], th_ss.at[0], th_rs.at[0], peer)
    theta_peer.start()

    def reduce_phase(phase, out, into, ss, rs):
        return [remote(out.at[1 + phase], into.at[1 + 3 * phase + d - 1], ss.at[1 + 3 * phase + d - 1], rs.at[1 + 3 * phase + d - 1],
                       (axis_peer(s, phase, d), c)) for d in (1, 2, 3)]

    theta_phases = [reduce_phase(a, thout, thin, th_ss, th_rs) for a in range(3)]
    final_phases = [reduce_phase(a, arout, arin, ar_ss, ar_rs) for a in range(3)]

    def theta_step(n):
        if n == 0:
            theta_peer.wait_recv()
            thout[1] = thout[0] + thin[0]
        else:
            for cp in theta_phases[n - 1]:
                cp.wait_recv()
            k = 1 + 3 * (n - 1)
            thout[1 + n] = thout[n] + ((thin[k] + thin[k + 1]) + thin[k + 2])
        if n < 3:
            for cp in theta_phases[n]:
                cp.start()

    def lanes_sum(x):
        return jnp.sum(x, axis=1, keepdims=True)

    def inner(x, y):
        return jnp.broadcast_to(lanes_sum(jnp.sum(x * y, axis=0)), (8, W))

    krylov[0] = b_ref[...]
    lane8 = lax.broadcasted_iota(jnp.int32, (8, W), 1)
    moments = jnp.zeros((8, W), F32)
    theta = None
    halo_copies, q_copies, p_copies = [], [], []
    for t in range(ITERS):
        hc = remote(krylov.at[t], halo.at[t], halo_ss.at[t], halo_rs.at[t], before)
        hc.start()
        halo_copies.append(hc)
        for j in range(ROWS):
            hi, lo = split(krylov[t, j])
            vs[j] = jnp.concatenate([hi.astype(F32), lo.astype(F32)], axis=0).astype(BF16)
        for r in range(ROWS):
            y = vs[r]
            out = jnp.dot(jnp.concatenate([y, y], axis=1), wt[r], preferred_element_type=F32)
            out = out[0:8] + out[8:16]
            for h in range(2):
                pair = jnp.concatenate([out[:, 256 * h:256 * h + W], out[:, 256 * h + W:256 * h + 2 * W]], axis=0)
                hi, lo = split(pair)
                at = (r * SLOTS + 2 * h) * 8
                bst[at:at + 16, 0:W] = hi
                bst[at:at + 16, W:2 * W] = lo
        spread = jnp.dot(gm[...], bst[...], preferred_element_type=F32)
        spread = (spread[:, :W] + spread[:, W:]).reshape(2 * ROWS, NRHS, W)
        qout[t] = spread[ROWS:]
        qc = remote(qout.at[t], qin.at[t], q_ss.at[t], q_rs.at[t], after)
        qc.start()
        q_copies.append(qc)
        if t == 0:
            sn_copy.start()
        pout[t] = spread[:ROWS] + dg[...] * krylov[t]
        for j in range(8):
            out = jnp.dot(vs[8 * c + j], dw[j], preferred_element_type=F32)
            out = out[0:8] + out[8:16]
            pout[t, 8 * c + j] = pout[t, 8 * c + j] + (out[:, :W] + out[:, W:])
        if t < 2:
            theta_step(2 * t)
        hc.wait_recv()
        for j in range(ROWS):
            hi, lo = split(halo[t, j])
            vs[ROWS + j] = jnp.concatenate([hi.astype(F32), lo.astype(F32)], axis=0).astype(BF16)
        for r in range(ROWS):
            x = jnp.concatenate([vs[jnp.clip(cols[r, k] - first, 0, 2 * ROWS - 1)] for k in range(SLOTS)], axis=1)
            out = lax.dot_general(x, wt[r], (((1,), (1,)), ((), ())), preferred_element_type=F32)
            out = out[0:8] + out[8:16]
            pout[t, r] = pout[t, r] + (out[:, :W] + out[:, W:])
        if t == 0:
            sn_copy.wait_recv()
            dg[...] = dg[...] + snin[...]
            pout[t] = pout[t] + snin[...] * krylov[t]
        qc.wait_recv()
        pout[t] = pout[t] + qin[t]
        pc = remote(pout.at[t], pin.at[t], peer_ss.at[t], peer_rs.at[t], peer)
        pc.start()
        p_copies.append(pc)
        if t < 2:
            theta_step(2 * t + 1)
        if t == 1:
            theta = thout[4] * (1.0 / (SLABS * ROWS * W))
        pc.wait_recv()
        image = pout[t] + pin[t]
        if t == 0:
            krylov[1] = image
        elif t == 1:
            hc.wait_send()
            plain = krylov[1]
            one = plain - theta * krylov[0]
            krylov[1] = one
            krylov[2] = image - theta * (plain + one)
            pairs = [(0, 0), (0, 1), (1, 1), (1, 2), (2, 2)]
        else:
            krylov[t + 1] = image - theta * krylov[t]
            pairs = [(t, t + 1), (t + 1, t + 1)][:1 if t == 3 else 2]
        if t >= 1:
            for i, j in pairs:
                moments = jnp.where(lane8 == i + j, inner(krylov[i], krylov[j]), moments)

    arout[1] = moments
    for a in range(3):
        for cp in final_phases[a]:
            cp.start()
        for cp in final_phases[a]:
            cp.wait_recv()
        k = 1 + 3 * a
        arout[2 + a] = arout[1 + a] + ((arin[k] + arin[k + 1]) + arin[k + 2])
    summed = arout[4]
    m = [jnp.broadcast_to(summed[:, k:k + 1], (8, W)) for k in range(8)]

    def dot(p, q):
        n = {}
        for i, u in enumerate(p):
            for j, v in enumerate(q):
                n[i + j] = n[i + j] + u * v if i + j in n else u * v
        total = None
        for k, u in n.items():
            total = u * m[k] if total is None else total + u * m[k]
        return total

    one = jnp.ones((8, W), F32)
    res, direction, sol = [one], [one], []
    rr = m[0]
    for it in range(ITERS):
        n = len(direction)
        image = [theta * direction[0]] + [direction[i - 1] + theta * direction[i] for i in range(1, n)] + [direction[-1]]
        alpha = rr / dot(direction, image)
        sol = [(sol[i] + alpha * direction[i]) if i < len(sol) else alpha * direction[i] for i in range(n)]
        res = [(res[i] - alpha * image[i]) if i < len(res) else -alpha * image[i] for i in range(n + 1)]
        if it < ITERS - 1:
            new = dot(res, res)
            beta = new / rr
            direction = [(res[i] + beta * direction[i]) if i < n else res[i] for i in range(n + 1)]
            rr = new
    xs = sol[0] * krylov[0]
    rs = res[0] * krylov[0]
    for i in range(1, ITERS + 1):
        if i < ITERS:
            xs = xs + sol[i] * krylov[i]
        rs = rs + res[i] * krylov[i]
    x_ref[...] = xs
    r_ref[...] = rs

    sn_copy.wait_send()
    theta_peer.wait_send()
    for ph in theta_phases + final_phases:
        for cp in ph:
            cp.wait_send()
    for t in range(ITERS):
        if t != 1:
            halo_copies[t].wait_send()
        q_copies[t].wait_send()
        p_copies[t].wait_send()


def body(right_side, diagonal, dense_blocks, tiles, tile_cols, tile_counts):
    vmem = pl.BlockSpec(memory_space=pltpu.VMEM)
    smem = pl.BlockSpec(memory_space=pltpu.SMEM)
    anym = pl.BlockSpec(memory_space=pl.ANY)
    vec = (ROWS, NRHS, W)
    dma = pltpu.SemaphoreType.DMA
    out = jax.ShapeDtypeStruct(vec, F32)
    return pl.pallas_call(
        kernel,
        out_shape=(out, out),
        in_specs=[smem, smem, vmem, vmem, anym, anym],
        out_specs=(vmem, vmem),
        scratch_shapes=[
            pltpu.VMEM((ROWS, SLOTS, W, W), F32),
            pltpu.VMEM((8, W, W), F32),
            pltpu.VMEM((ROWS, 2 * W, SLOTS * W), BF16),
            pltpu.VMEM((8, W, 2 * W), BF16),
            pltpu.VMEM((2 * ROWS * NRHS, 512), BF16),
            pltpu.VMEM((64, 8, W), F32),
            pltpu.VMEM((64, 8, W), F32),
            pltpu.VMEM((ITERS + 1,) + vec, F32),
            pltpu.VMEM((ITERS,) + vec, F32),
            pltpu.VMEM((ITERS,) + vec, F32),
            pltpu.VMEM((ITERS,) + vec, F32),
            pltpu.VMEM((ITERS,) + vec, F32),
            pltpu.VMEM((ITERS,) + vec, F32),
            pltpu.VMEM(vec, F32),
            pltpu.VMEM(vec, F32),
            pltpu.VMEM(vec, F32),
            pltpu.VMEM((2 * ROWS, 16, W), BF16),
            pltpu.VMEM((512, 2 * W), BF16),
            pltpu.VMEM((5, 8, W), F32),
            pltpu.VMEM((10, 8, W), F32),
            pltpu.VMEM((5, 8, W), F32),
            pltpu.VMEM((10, 8, W), F32),
            dma((4,)),
            dma,
            dma((ITERS,)),
            dma((ITERS,)),
            dma((ITERS,)),
            dma((ITERS,)),
            dma((ITERS,)),
            dma((ITERS,)),
            dma,
            dma,
            dma((10,)),
            dma((10,)),
            dma((10,)),
            dma((10,)),
        ],
        compiler_params=pltpu.CompilerParams(collective_id=0, has_side_effects=True, vmem_limit_bytes=40 << 20),
    )(tile_cols, tile_counts, right_side, diagonal, dense_blocks, tiles)


def solution(mesh):
    return jax.shard_map(
        body,
        mesh=mesh,
        in_specs=(
            P("slab", None, None),
            P("slab", None),
            P(("slab", "sub"), None, None),
            P("slab", "sub", None, None),
            P("slab", "sub"),
            P("slab"),
        ),
        out_specs=(P("slab", None, None), P("slab", None, None)),
        check_vma=False,
    )
```

time: 1430 us -> 60.3 us (0.04)
  blocking collectives: 1230 us -> 0 us
  waiting for transfers between devices: 107 us -> 0 us
  Pallas kernels: 0 us -> 51.9 us
  matrix products: 37.3 us -> 0 us
  starting transfers between devices: 21.6 us -> 0 us
    psum x7 -> x0, blocking collectives: 1230 us -> none  [the longest x4 694 us: squares(): return lax.psum(inner(residual, residual), 'slab')]
    psum x4 -> x0, waiting for transfers between devices: 87.5 us -> none  [body(): image = lax.psum(partial_image, 'sub') + diagonal[:, None, :] * direction]
    pallas_call x0 -> x1, Pallas kernels: none -> 51.9 us  [body(): pl.pallas_call(kernel, out_shape=(out, out), in_specs=[smem, smem, vmem,...]
    dot_general x20 -> x0, matrix products: 37.3 us -> none  [the longest x4 15.9 us: body(): jnp.einsum('ikab,isa->iksb', tiles, direction, precision=lax.Precision.HI...]
    ppermute x8 -> x0, starting transfers between devices: 21.4 us -> none  [from_behind(): return lax.ppermute(array, axis, pairs)]
    ppermute x8 -> x0, waiting for transfers between devices: 19 us -> none  [from_behind(): return lax.ppermute(array, axis, pairs)]
  transfers between devices with their start and end apart: 12 -> 0, of which waited for: 12 -> 0; matrix products, arithmetic and copies ran while one was open for 1% -> 0% of each run, Pallas kernels for 0% -> 0%
where the time goes in v1:
time: 60.3 us; the launch traced here: 60 us
  Pallas kernels  51.9 us (86%)
  local copies, waits for them, and re-layouts  7.44 us (12%)
  between operations  0.64 us (1%)
    pallas_call x1, Pallas kernels, body(): pl.pallas_call(kernel, out_shape=(out, out), in_specs=[smem, smem, vmem,...  51.9 us
    unnamed x13, local copies, waits for them, and re-layouts  7.44 us

profile of v1, /device:TPU:0, one launch (start us, length us, event | category | flops | bytes accessed | tf_op | source)
XLA Modules:
  0.0 60.0 jit_solution(13627879933354971276)
XLA Ops:
  0.6 0.8 %copy.8.cols = s32[16,4]{1,0:T(8,128)S(1)} copy(s32[16,4]{0,1:T(4,128)} %param.10) | data formatting | bytes 512 | tf_op args[4]
  1.4 0.0 copy-start
  1.4 2.2 %copy-done = f32[16,4,128,128]{3,2,1,0:T(8,128)S(1)} copy-done((f32[16,4,128,128]{3,2,1,0:T(8,128)S(1)}, f32[16,4,128,128]{3,2,1,0:T(8,128)}, u32[]{:S(2)}) %copy-start) | copy-done | bytes 4194328
  3.6 0.0 copy-start.1
  3.6 1.0 %copy-done.1 = f32[8,128,128]{2,1,0:T(8,128)S(1)} copy-done((f32[8,128,128]{2,1,0:T(8,128)S(1)}, f32[8,128,128]{2,1,0:T(8,128)}, u32[]{:S(2)}) %copy-start.1) | copy-done | bytes 524312
  4.6 0.0 copy-start.2
  4.6 0.8 %copy-done.2 = f32[16,8,128]{2,1,0:T(8,128)S(1)} copy-done((f32[16,8,128]{2,1,0:T(8,128)S(1)}, f32[16,8,128]{2,1,0:T(8,128)}, u32[]{:S(2)}) %copy-start.2) | copy-done | bytes 65560
  5.5 0.0 copy-start.3
  5.5 0.7 %copy-done.3 = f32[16,128]{1,0:T(8,128)S(1)} copy-done((f32[16,128]{1,0:T(8,128)S(1)}, f32[16,128]{1,0:T(8,128)}, u32[]{:S(2)}) %copy-start.3) | copy-done | bytes 8216
  6.2 0.0 copy-start.4
  6.2 0.7 %copy-done.4 = s32[16]{0:T(128)S(1)} copy-done((s32[16]{0:T(128)S(1)}, s32[16]{0:T(128)}, u32[]{:S(2)}) %copy-start.4) | copy-done | bytes 88
  6.8 51.9 %shard_map.77 = (f32[16,8,128]{2,1,0:T(8,128)S(1)}, f32[16,8,128]{2,1,0:T(8,128)S(1)}) custom-call(s32[16,4]{1,0:T(8,128)S(1)} %copy.8.cols, s32[16]{0:T(128)S(1)} %copy-done.4, f32[16,8,128]{2,1,0:T(8,128)S(1)} %copy-done.2, f32[16,128]{1,0:T(8,128)S(1)} %copy-done.3, f32[8,128,128]{2,1,0:T(8,128)S(1)} %copy-done.1, f32[16,4,128,128]{3,2,1,0:T(8,128)S(1)} %copy-done), custom_call_target="tpu_custom_call" | custom-call | tf_op jit(solution)/shard_map/pallas_call | solution.py:299
  58.8 0.6 %copy.11 = f32[16,8,128]{2,1,0:T(8,128)} copy(f32[16,8,128]{2,1,0:T(8,128)S(1)} %get-tuple-element.4) | data formatting | bytes 131072
  59.4 0.6 %copy.12 = f32[16,8,128]{2,1,0:T(8,128)} copy(f32[16,8,128]{2,1,0:T(8,128)S(1)} %get-tuple-element.5) | data formatting | bytes 131072
Async XLA Ops:
  1.4 2.2 %copy-start = (f32[16,4,128,128]{3,2,1,0:T(8,128)S(1)}, f32[16,4,128,128]{3,2,1,0:T(8,128)}, u32[]{:S(2)}) copy-start(f32[16,4,128,128]{3,2,1,0:T(8,128)} %tiles_hbm.1) | copy-start | bytes 12582916
  3.6 1.0 %copy-start.1 = (f32[8,128,128]{2,1,0:T(8,128)S(1)}, f32[8,128,128]{2,1,0:T(8,128)}, u32[]{:S(2)}) copy-start(f32[8,128,128]{2,1,0:T(8,128)} %dense_hbm.1) | copy-start | bytes 1572868
  4.6 0.8 %copy-start.2 = (f32[16,8,128]{2,1,0:T(8,128)S(1)}, f32[16,8,128]{2,1,0:T(8,128)}, u32[]{:S(2)}) copy-start(f32[16,8,128]{2,1,0:T(8,128)} %b_ref.1) | copy-start | bytes 196612
  5.5 0.7 %copy-start.3 = (f32[16,128]{1,0:T(8,128)S(1)}, f32[16,128]{1,0:T(8,128)}, u32[]{:S(2)}) copy-start(f32[16,128]{1,0:T(8,128)} %diag_ref.1) | copy-start | bytes 24580
  6.2 0.7 %copy-start.4 = (s32[16]{0:T(128)S(1)}, s32[16]{0:T(128)}, u32[]{:S(2)}) copy-start(s32[16]{0:T(128)} %counts.1) | copy-start | bytes 196

commit v2 on v1

v2 whole, which is shorter than its diff:
```python
import functools
import jax
import jax.numpy as jnp
from jax import lax
from jax.experimental import pallas as pl
from jax.experimental.pallas import tpu as pltpu
from jax.sharding import PartitionSpec as P

MESH = pl.DeviceIdType.MESH
F32 = jnp.float32
BF16 = jnp.bfloat16
ITERS = 4
ROWS = 16
SLOTS = 4
NRHS = 8
W = 128
SLABS = 64


def split(x):
    hi = x.astype(BF16)
    return hi, (x - hi.astype(F32)).astype(BF16)


def kernel(cols_hbm, counts_hbm, b_hbm, diag_hbm, dense_hbm, tiles_hbm, x_ref, r_ref,
           cols, counts, diag_ref, tf, df, wt, dw, gm, sq, krylov, halo, qout, qin, pout, pin, dg, snout, snin, vs, bst,
           pair_out, pair_in, all_in, in_sem, tile_sem, peer_ss, peer_rs, halo_ss, halo_rs, q_ss, q_rs, sn_ss, sn_rs, pair_ss, pair_rs, all_ss, all_rs):
    s = lax.axis_index("slab")
    c = lax.axis_index("sub")
    after = ((s + 1) % SLABS, c)
    before = ((s + SLABS - 1) % SLABS, c)
    peer = (s, 1 - c)
    first = s * ROWS

    small_copies = [pltpu.make_async_copy(a, b, in_sem.at[i]) for i, (a, b) in enumerate(
        [(cols_hbm, cols), (counts_hbm, counts), (b_hbm, krylov.at[0]), (diag_hbm, diag_ref), (dense_hbm, df)])]
    tile_copies = [pltpu.make_async_copy(tiles_hbm.at[pl.ds(4 * i, 4)], tf.at[pl.ds(4 * i, 4)], tile_sem.at[i]) for i in range(4)]
    for cp in small_copies[:3] + tile_copies + small_copies[3:]:
        cp.start()

    barrier = pltpu.get_barrier_semaphore()
    pl.semaphore_signal(barrier, inc=1, device_id=peer, device_id_type=MESH)

    def greet(d, carry):
        pl.semaphore_signal(barrier, inc=1, device_id=((s + d) % SLABS, c), device_id_type=MESH)
        return carry

    lax.fori_loop(1, SLABS, greet, 0, unroll=True)

    def remote(src, dst, ss, rs, dev):
        return pltpu.make_async_remote_copy(src_ref=src, dst_ref=dst, send_sem=ss, recv_sem=rs, device_id=dev, device_id_type=MESH)

    small_copies[0].wait()
    small_copies[1].wait()
    lane = lax.broadcasted_iota(jnp.int32, (8, W), 1)
    col_lanes = []
    for g in range(4):
        cv = jnp.zeros((8, W), jnp.int32)
        for u in range(16):
            t = g * 16 + u
            cv = jnp.where(lane // 8 == u, cols[t % SLOTS, t // SLOTS] - first, cv)
        col_lanes.append(cv)
    cv = jnp.concatenate(col_lanes, axis=1)
    sub_of = lax.broadcasted_iota(jnp.int32, (8, 512), 0)
    lane_of = lax.broadcasted_iota(jnp.int32, (8, 512), 1)
    cv = jnp.where(lane_of % 8 == sub_of, cv, -1)
    for j in range(0, 2 * ROWS, 2):
        top = jnp.where(cv == j, 1.0, 0.0)
        low = jnp.where(cv == j + 1, 1.0, 0.0)
        gm[8 * j:8 * j + 16, :] = jnp.concatenate([top, low], axis=0).astype(BF16)

    def own_parts(t):
        for j in range(ROWS):
            hi, lo = split(krylov[t, j])
            vs[j] = jnp.concatenate([hi.astype(F32), lo.astype(F32)], axis=0).astype(BF16)

    small_copies[2].wait()
    own_parts(0)

    for i in range(4):
        tile_copies[i].wait()

        def prep(rr, carry):
            r = 4 * i + rr
            for k in range(SLOTS):
                live = jnp.where(c * SLOTS + k < counts[r], 1.0, 0.0).astype(F32)
                t = tf[r, k] * live
                hi, lo = split(t)
                wt[r, 0:W, W * k:W * k + W] = hi
                wt[r, W:2 * W, W * k:W * k + W] = lo
                sq[r * SLOTS + k] = jnp.sum((t * t).reshape(16, 8, W), axis=0)
            return carry

        lax.fori_loop(0, 4, prep, 0, unroll=True)

    pl.semaphore_wait(barrier, SLABS)

    def spread_q(t):
        for r in range(ROWS):
            y = vs[r]
            out = jnp.dot(jnp.concatenate([y, y], axis=1), wt[r], preferred_element_type=F32)
            out = out[0:8] + out[8:16]
            for h in range(2):
                pair = jnp.concatenate([out[:, 256 * h:256 * h + W], out[:, 256 * h + W:256 * h + 2 * W]], axis=0)
                hi, lo = split(pair)
                at = (r * SLOTS + 2 * h) * 8
                bst[at:at + 16, 0:W] = hi
                bst[at:at + 16, W:2 * W] = lo
        spread = jnp.dot(gm[...], bst[...], preferred_element_type=F32)
        spread = (spread[:, :W] + spread[:, W:]).reshape(2 * ROWS, NRHS, W)
        qout[t] = spread[ROWS:]
        pout[t] = spread[:ROWS]

    halo_copies = [remote(krylov.at[t], halo.at[t], halo_ss.at[t], halo_rs.at[t], before) for t in range(ITERS)]
    q_copies = [remote(qout.at[t], qin.at[t], q_ss.at[t], q_rs.at[t], after) for t in range(ITERS)]
    p_copies = [remote(pout.at[t], pin.at[t], peer_ss.at[t], peer_rs.at[t], peer) for t in range(ITERS)]
    sn_copy = remote(snout, snin, sn_ss, sn_rs, after)
    pair_copies = [remote(pair_out.at[i], pair_in.at[i], pair_ss.at[i], pair_rs.at[i], peer) for i in range(2)]

    def all_start(i):
        pair_copies[i].wait_recv()
        pair_out[2 + i, 0:1] = pair_out[i, 0:1] + pair_in[i, 0:1]

        def send(d, carry):
            remote(pair_out.at[2 + i, pl.ds(0, 1)], all_in.at[i, d - 1], all_ss.at[i], all_rs.at[i], ((s + d) % SLABS, c)).start()
            return carry

        lax.fori_loop(1, SLABS, send, 0, unroll=True)

    def all_copy(i):
        return remote(all_in.at[i], all_in.at[i], all_ss.at[i], all_rs.at[i], peer)

    def all_done(i):
        all_copy(i).wait_recv()
        return pair_out[2 + i, 0:1] + jnp.sum(all_in[i], axis=0)

    halo_copies[0].start()
    spread_q(0)
    q_copies[0].start()

    sigma = jnp.broadcast_to(jnp.sqrt(jnp.sum(jnp.sum(sq[...], axis=2, keepdims=True), axis=1, keepdims=True)), (64, 8, W))
    sigma2 = sigma.reshape(512, W)
    s_hi = sigma2.astype(BF16)
    rest = sigma2 - s_hi.astype(F32)
    s_mid = rest.astype(BF16)
    s_lo = (rest - s_mid.astype(F32)).astype(BF16)
    scol = jnp.dot(gm[...], jnp.concatenate([s_hi, s_mid], axis=1), preferred_element_type=F32)
    scol = scol[:, :W] + scol[:, W:] + jnp.dot(gm[...], s_lo, preferred_element_type=F32)
    scol = scol.reshape(2 * ROWS, NRHS, W)
    snout[...] = scol[ROWS:]
    sn_copy.start()

    small_copies[3].wait()
    small_copies[4].wait()
    dsum = jnp.zeros((8, W), F32)
    dsig = []
    for j in range(8):
        d = df[j]
        sqd = jnp.sum((d * d).reshape(16, 8, W), axis=0)
        dtot = jnp.sum(jnp.sum(sqd, axis=1, keepdims=True), axis=0, keepdims=True)
        ds = jnp.broadcast_to(jnp.sqrt(dtot), (8, W))
        dsig.append(ds)
        dsum = dsum + ds
    half = 0.5 * diag_ref[...]
    diag_sum = jnp.sum(jnp.sum(half, axis=0, keepdims=True), axis=1, keepdims=True)
    pair_out[0] = (2.0 * jnp.sum(sigma, axis=0) + dsum) * W + diag_sum
    pair_copies[0].start()
    for j in range(8):
        d = df[j]
        hi, lo = split(0.5 * (d + d.T))
        dw[j, :, 0:W] = hi
        dw[j, :, W:2 * W] = lo
    dg[...] = jnp.sum(sigma.reshape(ROWS, SLOTS, 8, W), axis=1) + scol[:ROWS] + half[:, None, :]
    for j in range(8):
        dg[8 * c + j] = dg[8 * c + j] + dsig[j]

    sub8 = lax.broadcasted_iota(jnp.int32, (8, W), 0)

    def place(k, x, row):
        return jnp.where(lane == 8 * sub8 + k, jnp.sum(x, axis=1, keepdims=True), row)

    def inner(i, j):
        return jnp.sum(krylov[i] * krylov[j], axis=0)

    def local_part(t):
        loc = [dg[r] * krylov[t, r] for r in range(ROWS)]
        for r in range(ROWS):
            pout[t, r] = pout[t, r] + loc[r]
        seen = loc[0] * krylov[t, 0]
        for r in range(1, ROWS):
            seen = seen + loc[r] * krylov[t, r]
        for j in range(8):
            out = jnp.dot(vs[8 * c + j], dw[j], preferred_element_type=F32)
            out = out[0:8] + out[8:16]
            out = out[:, :W] + out[:, W:]
            pout[t, 8 * c + j] = pout[t, 8 * c + j] + out
            seen = seen + out * krylov[t, 8 * c + j]
        return seen

    def forward(t):
        for j in range(ROWS):
            hi, lo = split(halo[t, j])
            vs[ROWS + j] = jnp.concatenate([hi.astype(F32), lo.astype(F32)], axis=0).astype(BF16)
        seen = jnp.zeros((8, W), F32)
        for r in range(ROWS):
            x = jnp.concatenate([vs[jnp.clip(cols[k, r] - first, 0, 2 * ROWS - 1)] for k in range(SLOTS)], axis=1)
            out = lax.dot_general(x, wt[r], (((1,), (1,)), ((), ())), preferred_element_type=F32)
            out = out[0:8] + out[8:16]
            out = out[:, :W] + out[:, W:]
            pout[t, r] = pout[t, r] + out
            seen = seen + out * krylov[t, r]
        return seen

    moments = jnp.zeros((8, W), F32)
    theta = None
    for t in range(ITERS):
        if t > 0:
            halo_copies[t].start()
            own_parts(t)
            spread_q(t)
            q_copies[t].start()
        seen = local_part(t)
        if t == 2:
            for i, j in [(0, 0), (0, 1), (1, 1), (1, 2), (2, 2)]:
                moments = place(i + j, inner(i, j), moments)
        if t == 3:
            for i, j in [(2, 3), (3, 3)]:
                moments = place(i + j, inner(i, j), moments)
        if t == 0:
            all_start(0)
        halo_copies[t].wait_recv()
        crossed = forward(t)
        if t == 3:
            row = 0.5 * moments + place(7, seen + 2.0 * crossed, jnp.zeros((8, W), F32))
            pair_out[1] = jnp.broadcast_to(jnp.sum(row, axis=0, keepdims=True), (8, W))
            pair_copies[1].start()
        if t == 0:
            sn_copy.wait_recv()
            dg[...] = dg[...] + snin[...]
            pout[t] = pout[t] + snin[...] * krylov[t]
        q_copies[t].wait_recv()
        pout[t] = pout[t] + qin[t]
        p_copies[t].start()
        if t == 3:
            all_start(1)
        if t == 1:
            theta = jnp.broadcast_to(all_done(0) * (1.0 / (SLABS * ROWS * W)), (8, W))
            dg[...] = dg[...] - 0.5 * theta
        p_copies[t].wait_recv()
        image = pout[t] + pin[t]
        if t == 1:
            halo_copies[1].wait_send()
            plain = krylov[1]
            one = plain - theta * krylov[0]
            krylov[1] = one
            krylov[2] = image - theta * (plain + one)
        else:
            krylov[t + 1] = image

    summed = jnp.broadcast_to(all_done(1), (8, W))
    m = [jnp.broadcast_to(jnp.sum(jnp.where(lane == 8 * sub8 + k, summed, 0.0), axis=1, keepdims=True), (8, W)) for k in range(8)]

    def dot(p, q):
        n = {}
        for i, u in enumerate(p):
            for j, v in enumerate(q):
                n[i + j] = n[i + j] + u * v if i + j in n else u * v
        total = None
        for k, u in n.items():
            total = u * m[k] if total is None else total + u * m[k]
        return total

    one = jnp.ones((8, W), F32)
    res, direction, sol = [one], [one], []
    rr = m[0]
    for it in range(ITERS):
        n = len(direction)
        image = [theta * direction[0]] + [direction[i - 1] + theta * direction[i] for i in range(1, n)] + [direction[-1]]
        alpha = rr / dot(direction, image)
        sol = [(sol[i] + alpha * direction[i]) if i < len(sol) else alpha * direction[i] for i in range(n)]
        res = [(res[i] - alpha * image[i]) if i < len(res) else -alpha * image[i] for i in range(n + 1)]
        if it < ITERS - 1:
            new = dot(res, res)
            beta = new / rr
            direction = [(res[i] + beta * direction[i]) if i < n else res[i] for i in range(n + 1)]
            rr = new
    for j in range(ROWS):
        xs = sol[0] * krylov[0, j]
        rs = res[0] * krylov[0, j]
        for i in range(1, ITERS + 1):
            if i < ITERS:
                xs = xs + sol[i] * krylov[i, j]
            rs = rs + res[i] * krylov[i, j]
        x_ref[j] = xs
        r_ref[j] = rs

    sn_copy.wait_send()
    for i in range(2):
        pair_copies[i].wait_send()
        all_copy(i).wait_send()
    for t in range(ITERS):
        if t != 1:
            halo_copies[t].wait_send()
        q_copies[t].wait_send()
        p_copies[t].wait_send()


def body(right_side, diagonal, dense_blocks, tiles, tile_cols, tile_counts):
    vmem = pl.BlockSpec(memory_space=pltpu.VMEM)
    anym = pl.BlockSpec(memory_space=pl.ANY)
    vec = (ROWS, NRHS, W)
    dma = pltpu.SemaphoreType.DMA
    out = jax.ShapeDtypeStruct(vec, F32)
    return pl.pallas_call(
        kernel,
        out_shape=(out, out),
        in_specs=[anym] * 6,
        out_specs=(vmem, vmem),
        scratch_shapes=[
            pltpu.SMEM((SLOTS, ROWS), jnp.int32),
            pltpu.SMEM((ROWS,), jnp.int32),
            pltpu.VMEM((ROWS, W), F32),
            pltpu.VMEM((ROWS, SLOTS, W, W), F32),
            pltpu.VMEM((8, W, W), F32),
            pltpu.VMEM((ROWS, 2 * W, SLOTS * W), BF16),
            pltpu.VMEM((8, W, 2 * W), BF16),
            pltpu.VMEM((2 * ROWS * NRHS, 512), BF16),
            pltpu.VMEM((64, 8, W), F32),
            pltpu.VMEM((ITERS + 1,) + vec, F32),
            pltpu.VMEM((ITERS,) + vec, F32),
            pltpu.VMEM((ITERS,) + vec, F32),
            pltpu.VMEM((ITERS,) + vec, F32),
            pltpu.VMEM((ITERS,) + vec, F32),
            pltpu.VMEM((ITERS,) + vec, F32),
            pltpu.VMEM(vec, F32),
            pltpu.VMEM(vec, F32),
            pltpu.VMEM(vec, F32),
            pltpu.VMEM((2 * ROWS, 16, W), BF16),
            pltpu.VMEM((512, 2 * W), BF16),
            pltpu.VMEM((4, 8, W), F32),
            pltpu.VMEM((2, 8, W), F32),
            pltpu.VMEM((2, SLABS - 1, 1, W), F32),
            dma((5,)),
            dma((4,)),
            dma((ITERS,)),
            dma((ITERS,)),
            dma((ITERS,)),
            dma((ITERS,)),
            dma((ITERS,)),
            dma((ITERS,)),
            dma,
            dma,
            dma((2,)),
            dma((2,)),
            dma((2,)),
            dma((2,)),
        ],
        compiler_params=pltpu.CompilerParams(collective_id=0, has_side_effects=True, vmem_limit_bytes=60 << 20),
    )(tile_cols.T, tile_counts, right_side, diagonal, dense_blocks, tiles)


def solution(mesh):
    return jax.shard_map(
        body,
        mesh=mesh,
        in_specs=(
            P("slab", None, None),
            P("slab", None),
            P(("slab", "sub"), None, None),
            P("slab", "sub", None, None),
            P("slab", "sub"),
            P("slab"),
        ),
        out_specs=(P("slab", None, None), P("slab", None, None)),
        check_vma=False,
    )
```

time: 60.3 us -> 51.6 us (0.86)
  local copies, waits for them, and re-layouts: 7.44 us -> 2.95 us
  Pallas kernels: 51.9 us -> 47.5 us
    unnamed x13 -> x2, local copies, waits for them, and re-layouts: 7.44 us -> 2.95 us
    pallas_call x1, Pallas kernels: 51.9 us -> 47.5 us  [body(): pl.pallas_call(kernel, out_shape=(out, out), in_specs=[anym] * 6, out_spe...]
where the time goes in v2:
time: 51.6 us; the launch traced here: 51.1 us
  Pallas kernels  47.5 us (92%)
  local copies, waits for them, and re-layouts  2.95 us (6%)
  between operations  0.64 us (1%)
    pallas_call x1, Pallas kernels, body(): pl.pallas_call(kernel, out_shape=(out, out), in_specs=[anym] * 6, out_spe...  47.5 us
    unnamed x2, local copies, waits for them, and re-layouts  2.95 us

profile of v2, /device:TPU:0, one launch (start us, length us, event | category | flops | bytes accessed | tf_op | source)
XLA Modules:
  0.0 51.1 jit_solution(16260847591129401257)
XLA Ops:
  0.6 47.5 %shard_map.77 = (f32[16,8,128]{2,1,0:T(8,128)}, f32[16,8,128]{2,1,0:T(8,128)}) custom-call(s32[4,16]{1,0:T(4,128)} %bitcast.1, s32[16]{0:T(128)} %counts_hbm.1, f32[16,8,128]{2,1,0:T(8,128)} %b_hbm.1, f32[16,128]{1,0:T(8,128)} %diag_hbm.1, f32[8,128,128]{2,1,0:T(8,128)} %dense_hbm.1, f32[16,4,128,128]{3,2,1,0:T(8,128)} %tiles_hbm.1), custom_call_target="tpu_custom_call" | custom-call | tf_op jit(solution)/shard_map/pallas_call | solution.py:314
  48.2 1.5 %copy.10 = f32[16,8,128]{2,1,0:T(8,128)} copy(f32[16,8,128]{2,1,0:T(8,128)} %get-tuple-element.4) | data formatting | bytes 131072
  49.6 1.5 %copy.11 = f32[16,8,128]{2,1,0:T(8,128)} copy(f32[16,8,128]{2,1,0:T(8,128)} %get-tuple-element.5) | data formatting | bytes 131072

commit v3 on v2

--- a/solution.py
+++ b/solution.py
@@ -22,13 +22,13 @@
     return hi, (x - hi.astype(F32)).astype(BF16)
 
 
-def kernel(cols_hbm, counts_hbm, b_hbm, diag_hbm, dense_hbm, tiles_hbm, x_ref, r_ref,
-           cols, counts, diag_ref, tf, df, wt, dw, gm, sq, krylov, halo, qout, qin, pout, pin, dg, snout, snin, vs, bst,
-           pair_out, pair_in, all_in, in_sem, tile_sem, peer_ss, peer_rs, halo_ss, halo_rs, q_ss, q_rs, sn_ss, sn_rs, pair_ss, pair_rs, all_ss, all_rs):
+def kernel(cols_hbm, counts_hbm, b_hbm, diag_hbm, dense_hbm, tiles_hbm, basis_hbm, sol_ref, res_ref,
+           cols, counts, diag_ref, tf, df, wt, wf, dw, gm, sq, krylov, halo, qout, qin, pout, pin, dg, snout, snin, vs, bst,
+           pair_out, pair_in, all_in, in_sem, out_sem, tile_sem, peer_ss, peer_rs, halo_ss, halo_rs, q_ss, q_rs, sn_ss, sn_rs, pair_ss, pair_rs, all_ss, all_rs):
     s = lax.axis_index("slab")
     c = lax.axis_index("sub")
-    after = ((s + 1) % SLABS, c)
-    before = ((s + SLABS - 1) % SLABS, c)
+    after = ((s + 1) % SLABS, 1 - c)
+    before = ((s + SLABS - 1) % SLABS, 1 - c)
     peer = (s, 1 - c)
     first = s * ROWS
 
@@ -39,7 +39,8 @@
         cp.start()
 
     barrier = pltpu.get_barrier_semaphore()
-    pl.semaphore_signal(barrier, inc=1, device_id=peer, device_id_type=MESH)
+    for dev in (peer, after, before):
+        pl.semaphore_signal(barrier, inc=1, device_id=dev, device_id_type=MESH)
 
     def greet(d, carry):
         pl.semaphore_signal(barrier, inc=1, device_id=((s + d) % SLABS, c), device_id_type=MESH)
@@ -77,11 +78,26 @@
     small_copies[2].wait()
     own_parts(0)
 
+    def back(r):
+        y = vs[r]
+        out = jnp.dot(jnp.concatenate([y, y], axis=1), wt[r], preferred_element_type=F32)
+        out = out[0:8] + out[8:16]
+        for h in range(2):
+            pair = jnp.concatenate([out[:, 256 * h:256 * h + W], out[:, 256 * h + W:256 * h + 2 * W]], axis=0)
+            hi, lo = split(pair)
+            at = (r * SLOTS + 2 * h) * 8
+            bst[at:at + 16, 0:W] = hi
+            bst[at:at + 16, W:2 * W] = lo
+
+    def spread_q(t):
+        spread = jnp.dot(gm[...], bst[...], preferred_element_type=F32)
+        spread = (spread[:, :W] + spread[:, W:]).reshape(2 * ROWS, NRHS, W)
+        qout[t] = spread[ROWS:]
+        pout[t] = spread[:ROWS]
+
     for i in range(4):
         tile_copies[i].wait()
-
-        def prep(rr, carry):
-            r = 4 * i + rr
+        for r in range(4 * i, 4 * i + 4):
             for k in range(SLOTS):
                 live = jnp.where(c * SLOTS + k < counts[r], 1.0, 0.0).astype(F32)
                 t = tf[r, k] * live
@@ -89,27 +105,9 @@
                 wt[r, 0:W, W * k:W * k + W] = hi
                 wt[r, W:2 * W, W * k:W * k + W] = lo
                 sq[r * SLOTS + k] = jnp.sum((t * t).reshape(16, 8, W), axis=0)
-            return carry
-
-        lax.fori_loop(0, 4, prep, 0, unroll=True)
-
-    pl.semaphore_wait(barrier, SLABS)
-
-    def spread_q(t):
-        for r in range(ROWS):
-            y = vs[r]
-            out = jnp.dot(jnp.concatenate([y, y], axis=1), wt[r], preferred_element_type=F32)
-            out = out[0:8] + out[8:16]
-            for h in range(2):
-                pair = jnp.concatenate([out[:, 256 * h:256 * h + W], out[:, 256 * h + W:256 * h + 2 * W]], axis=0)
-                hi, lo = split(pair)
-                at = (r * SLOTS + 2 * h) * 8
-                bst[at:at + 16, 0:W] = hi
-                bst[at:at + 16, W:2 * W] = lo
-        spread = jnp.dot(gm[...], bst[...], preferred_element_type=F32)
-        spread = (spread[:, :W] + spread[:, W:]).reshape(2 * ROWS, NRHS, W)
-        qout[t] = spread[ROWS:]
-        pout[t] = spread[:ROWS]
+            back(r)
+    spread_q(0)
+    pl.semaphore_wait(barrier, SLABS + 2)
 
     halo_copies = [remote(krylov.at[t], halo.at[t], halo_ss.at[t], halo_rs.at[t], before) for t in range(ITERS)]
     q_copies = [remote(qout.at[t], qin.at[t], q_ss.at[t], q_rs.at[t], after) for t in range(ITERS)]
@@ -135,7 +133,6 @@
         return pair_out[2 + i, 0:1] + jnp.sum(all_in[i], axis=0)
 
     halo_copies[0].start()
-    spread_q(0)
     q_copies[0].start()
 
     sigma = jnp.broadcast_to(jnp.sqrt(jnp.sum(jnp.sum(sq[...], axis=2, keepdims=True), axis=1, keepdims=True)), (64, 8, W))
@@ -204,19 +201,22 @@
         seen = jnp.zeros((8, W), F32)
         for r in range(ROWS):
             x = jnp.concatenate([vs[jnp.clip(cols[k, r] - first, 0, 2 * ROWS - 1)] for k in range(SLOTS)], axis=1)
-            out = lax.dot_general(x, wt[r], (((1,), (1,)), ((), ())), preferred_element_type=F32)
+            out = jnp.dot(x, wf[r], preferred_element_type=F32)
             out = out[0:8] + out[8:16]
             out = out[:, :W] + out[:, W:]
             pout[t, r] = pout[t, r] + out
             seen = seen + out * krylov[t, r]
         return seen
 
+    basis_copies = [pltpu.make_async_copy(krylov.at[i], basis_hbm.at[i], out_sem.at[i]) for i in range(ITERS + 1)]
     moments = jnp.zeros((8, W), F32)
     theta = None
     for t in range(ITERS):
         if t > 0:
             halo_copies[t].start()
             own_parts(t)
+            for r in range(ROWS):
+                back(r)
             spread_q(t)
             q_copies[t].start()
         seen = local_part(t)
@@ -227,7 +227,11 @@
             for i, j in [(2, 3), (3, 3)]:
                 moments = place(i + j, inner(i, j), moments)
         if t == 0:
+            for r in range(8):
+                wf[r] = wt[r].T
             all_start(0)
+            for r in range(8, ROWS):
+                wf[r] = wt[r].T
         halo_copies[t].wait_recv()
         crossed = forward(t)
         if t == 3:
@@ -254,8 +258,12 @@
             one = plain - theta * krylov[0]
             krylov[1] = one
             krylov[2] = image - theta * (plain + one)
+            basis_copies[0].start()
+            basis_copies[1].start()
         else:
             krylov[t + 1] = image
+        if t > 0:
+            basis_copies[t + 1].start()
 
     summed = jnp.broadcast_to(all_done(1), (8, W))
     m = [jnp.broadcast_to(jnp.sum(jnp.where(lane == 8 * sub8 + k, summed, 0.0), axis=1, keepdims=True), (8, W)) for k in range(8)]
@@ -284,16 +292,14 @@
             beta = new / rr
             direction = [(res[i] + beta * direction[i]) if i < n else res[i] for i in range(n + 1)]
             rr = new
-    for j in range(ROWS):
-        xs = sol[0] * krylov[0, j]
-        rs = res[0] * krylov[0, j]
-        for i in range(1, ITERS + 1):
-            if i < ITERS:
-                xs = xs + sol[i] * krylov[i, j]
-            rs = rs + res[i] * krylov[i, j]
-        x_ref[j] = xs
-        r_ref[j] = rs
-
+    for i in range(ITERS):
+        sol_ref[i] = sol[i]
+    sol_ref[ITERS] = jnp.zeros((8, W), F32)
+    for i in range(ITERS + 1):
+        res_ref[i] = res[i]
+
+    for cp in basis_copies:
+        cp.wait()
     sn_copy.wait_send()
     for i in range(2):
         pair_copies[i].wait_send()
@@ -310,12 +316,12 @@
     anym = pl.BlockSpec(memory_space=pl.ANY)
     vec = (ROWS, NRHS, W)
     dma = pltpu.SemaphoreType.DMA
-    out = jax.ShapeDtypeStruct(vec, F32)
-    return pl.pallas_call(
+    coef = jax.ShapeDtypeStruct((ITERS + 1, NRHS, W), F32)
+    basis, sol, res = pl.pallas_call(
         kernel,
-        out_shape=(out, out),
+        out_shape=(jax.ShapeDtypeStruct((ITERS + 1,) + vec, F32), coef, coef),
         in_specs=[anym] * 6,
-        out_specs=(vmem, vmem),
+        out_specs=(anym, vmem, vmem),
         scratch_shapes=[
             pltpu.SMEM((SLOTS, ROWS), jnp.int32),
             pltpu.SMEM((ROWS,), jnp.int32),
@@ -323,6 +329,7 @@
             pltpu.VMEM((ROWS, SLOTS, W, W), F32),
             pltpu.VMEM((8, W, W), F32),
             pltpu.VMEM((ROWS, 2 * W, SLOTS * W), BF16),
+            pltpu.VMEM((ROWS, SLOTS * W, 2 * W), BF16),
             pltpu.VMEM((8, W, 2 * W), BF16),
             pltpu.VMEM((2 * ROWS * NRHS, 512), BF16),
             pltpu.VMEM((64, 8, W), F32),
@@ -341,6 +348,7 @@
             pltpu.VMEM((2, 8, W), F32),
             pltpu.VMEM((2, SLABS - 1, 1, W), F32),
             dma((5,)),
+            dma((ITERS + 1,)),
             dma((4,)),
             dma((ITERS,)),
             dma((ITERS,)),
@@ -357,6 +365,9 @@
         ],
         compiler_params=pltpu.CompilerParams(collective_id=0, has_side_effects=True, vmem_limit_bytes=60 << 20),
     )(tile_cols.T, tile_counts, right_side, diagonal, dense_blocks, tiles)
+    x = jnp.sum(sol[:, None] * basis, axis=0)
+    r = jnp.sum(res[:, None] * basis, axis=0)
+    return x, r
 
 
 def solution(mesh):

time: 51.6 us -> 48.1 us (0.932)
  local copies, waits for them, and re-layouts: 2.95 us -> 0 us
  Pallas kernels: 47.5 us -> 45.6 us
  other arithmetic: 0 us -> 1.7 us
    unnamed x2 -> x0, local copies, waits for them, and re-layouts: 2.95 us -> none
    pallas_call x1, Pallas kernels: 47.5 us -> 45.6 us  [body(): pl.pallas_call(kernel, out_shape=(jax.ShapeDtypeStruct((ITERS + 1,) + vec...]
    reduce_sum x0 -> x1, other arithmetic: none -> 1.7 us  [body(): r = jnp.sum(res[:, None] * basis, axis=0)]
where the time goes in v3:
time: 48.1 us; the launch traced here: 48 us
  Pallas kernels  45.6 us (95%)
  other arithmetic  1.7 us (4%)
  between operations  0.64 us (1%)
    pallas_call x1, Pallas kernels, body(): pl.pallas_call(kernel, out_shape=(jax.ShapeDtypeStruct((ITERS + 1,) + vec...  45.6 us
    reduce_sum x1, other arithmetic, body(): r = jnp.sum(res[:, None] * basis, axis=0)  1.7 us

profile of v3, /device:TPU:0, one launch (start us, length us, event | category | flops | bytes accessed | tf_op | source)
XLA Modules:
  0.0 48.0 jit_solution(9804146244350568463)
XLA Ops:
  0.6 45.6 %shard_map.77 = (f32[5,16,8,128]{3,2,1,0:T(8,128)}, f32[5,8,128]{2,1,0:T(8,128)}, f32[5,8,128]{2,1,0:T(8,128)}) custom-call(s32[4,16]{1,0:T(4,128)} %bitcast.1, s32[16]{0:T(128)} %counts_hbm.1, f32[16,8,128]{2,1,0:T(8,128)} %b_hbm.1, f32[16,128]{1,0:T(8,128)} %diag_hbm.1, f32[8,128,128]{2,1,0:T(8,128)} %dense_hbm.1, f32[16,4,128,128]{3,2,1,0:T(8,128)} %tiles_hbm.1), custom_call_target="tpu_custom_call" | custom-call | tf_op jit(solution)/shard_map/pallas_call | solution.py:320
  46.3 1.7 %multiply_reduce_fusion = (f32[16,8,128]{2,1,0:T(8,128)}, f32[16,8,128]{2,1,0:T(8,128)}) fusion(f32[5,16,8,128]{3,2,1,0:T(8,128)} %get-tuple-element.6, f32[5,8,128]{2,1,0:T(8,128)} %get-tuple-element.7, f32[5,8,128]{2,1,0:T(8,128)} %get-tuple-element.5), kind=kLoop, calls=%fused_computation | loop fusion | flops 294912 | bytes 499712 | tf_op jit(solution)/shard_map/reduce_sum | solution.py:369

commit v4 on v3

--- a/solution.py
+++ b/solution.py
@@ -22,9 +22,18 @@
     return hi, (x - hi.astype(F32)).astype(BF16)
 
 
-def kernel(cols_hbm, counts_hbm, b_hbm, diag_hbm, dense_hbm, tiles_hbm, basis_hbm, sol_ref, res_ref,
-           cols, counts, diag_ref, tf, df, wt, wf, dw, gm, sq, krylov, halo, qout, qin, pout, pin, dg, snout, snin, vs, bst,
-           pair_out, pair_in, all_in, in_sem, out_sem, tile_sem, peer_ss, peer_rs, halo_ss, halo_rs, q_ss, q_rs, sn_ss, sn_rs, pair_ss, pair_rs, all_ss, all_rs):
+def far(offset):
+    return (sum(v != 0 for v in offset), sum(min(v, 4 - v) for v in offset))
+
+
+CUBE = sorted([(a, b, d) for a in range(4) for b in range(4) for d in range(4) if (a, b, d) != (0, 0, 0)], key=far, reverse=True)
+PLANE = [o for o in CUBE if o[0] == 0]
+LINE = [o for o in CUBE if o[1] == 0 and o[2] == 0]
+
+
+def kernel(cols_hbm, counts_hbm, b_hbm, diag_hbm, dense_hbm, tiles_hbm, krylov, sol_ref, res_ref,
+           cols, counts, diag_ref, tf, df, wt, wf, dw, gm, sq, halo, qout, qin, pout, pin, dg, snout, snin, vs, bst,
+           pair_out, pair_in, all_in, plane_in, line_in, in_sem, tile_sem, peer_ss, peer_rs, halo_ss, halo_rs, q_ss, q_rs, sn_ss, sn_rs, pair_ss, pair_rs, row_ss, row_rs):
     s = lax.axis_index("slab")
     c = lax.axis_index("sub")
     after = ((s + 1) % SLABS, 1 - c)
@@ -42,11 +51,14 @@
     for dev in (peer, after, before):
         pl.semaphore_signal(barrier, inc=1, device_id=dev, device_id_type=MESH)
 
-    def greet(d, carry):
-        pl.semaphore_signal(barrier, inc=1, device_id=((s + d) % SLABS, c), device_id_type=MESH)
-        return carry
-
-    lax.fori_loop(1, SLABS, greet, 0, unroll=True)
+    z, xx, yy = s // 16, (s // 4) % 4, s % 4
+
+    def moved(offset):
+        a, b, d = offset
+        return (((z + a) % 4) * 16 + ((xx + b) % 4) * 4 + (yy + d) % 4, c)
+
+    for offset in CUBE:
+        pl.semaphore_signal(barrier, inc=1, device_id=moved(offset), device_id_type=MESH)
 
     def remote(src, dst, ss, rs, dev):
         return pltpu.make_async_remote_copy(src_ref=src, dst_ref=dst, send_sem=ss, recv_sem=rs, device_id=dev, device_id_type=MESH)
@@ -115,22 +127,26 @@
     sn_copy = remote(snout, snin, sn_ss, sn_rs, after)
     pair_copies = [remote(pair_out.at[i], pair_in.at[i], pair_ss.at[i], pair_rs.at[i], peer) for i in range(2)]
 
-    def all_start(i):
+    def pair_sum(i):
         pair_copies[i].wait_recv()
-        pair_out[2 + i, 0:1] = pair_out[i, 0:1] + pair_in[i, 0:1]
-
-        def send(d, carry):
-            remote(pair_out.at[2 + i, pl.ds(0, 1)], all_in.at[i, d - 1], all_ss.at[i], all_rs.at[i], ((s + d) % SLABS, c)).start()
-            return carry
-
-        lax.fori_loop(1, SLABS, send, 0, unroll=True)
-
-    def all_copy(i):
-        return remote(all_in.at[i], all_in.at[i], all_ss.at[i], all_rs.at[i], peer)
-
-    def all_done(i):
-        all_copy(i).wait_recv()
-        return pair_out[2 + i, 0:1] + jnp.sum(all_in[i], axis=0)
+        return pair_out[i, 0:1] + pair_in[i, 0:1]
+
+    def row_copies(src, into, i, offsets):
+        return [remote(src, into.at[pl.ds(n, 1)], row_ss.at[i], row_rs.at[i], moved(o)) for n, o in enumerate(offsets)]
+
+    def row_all(into, i, count):
+        return remote(into.at[pl.ds(0, count)], into.at[pl.ds(0, count)], row_ss.at[i], row_rs.at[i], peer)
+
+    def rows_start(k, row):
+        pair_out[2 + k, 0:1] = row
+        for cp in row_copies(pair_out.at[2 + k, pl.ds(0, 1)], (plane_in, line_in, all_in)[k], k, (PLANE, LINE, CUBE)[k]):
+            cp.start()
+
+    def rows_done(k):
+        into, count = ((plane_in, len(PLANE)), (line_in, len(LINE)), (all_in, len(CUBE)))[k]
+        row_all(into, k, count).wait_recv()
+        into[count:count + 1] = pair_out[2 + k, 0:1]
+        return jnp.sum(into[0:count + 1], axis=0, keepdims=True)
 
     halo_copies[0].start()
     q_copies[0].start()
@@ -208,7 +224,6 @@
             seen = seen + out * krylov[t, r]
         return seen
 
-    basis_copies = [pltpu.make_async_copy(krylov.at[i], basis_hbm.at[i], out_sem.at[i]) for i in range(ITERS + 1)]
     moments = jnp.zeros((8, W), F32)
     theta = None
     for t in range(ITERS):
@@ -229,7 +244,7 @@
         if t == 0:
             for r in range(8):
                 wf[r] = wt[r].T
-            all_start(0)
+            rows_start(0, pair_sum(0))
             for r in range(8, ROWS):
                 wf[r] = wt[r].T
         halo_copies[t].wait_recv()
@@ -246,9 +261,11 @@
         pout[t] = pout[t] + qin[t]
         p_copies[t].start()
         if t == 3:
-            all_start(1)
+            rows_start(2, pair_sum(1))
+        if t == 0:
+            rows_start(1, rows_done(0))
         if t == 1:
-            theta = jnp.broadcast_to(all_done(0) * (1.0 / (SLABS * ROWS * W)), (8, W))
+            theta = jnp.broadcast_to(rows_done(1) * (1.0 / (SLABS * ROWS * W)), (8, W))
             dg[...] = dg[...] - 0.5 * theta
         p_copies[t].wait_recv()
         image = pout[t] + pin[t]
@@ -258,14 +275,10 @@
             one = plain - theta * krylov[0]
             krylov[1] = one
             krylov[2] = image - theta * (plain + one)
-            basis_copies[0].start()
-            basis_copies[1].start()
         else:
             krylov[t + 1] = image
-        if t > 0:
-            basis_copies[t + 1].start()
-
-    summed = jnp.broadcast_to(all_done(1), (8, W))
+
+    summed = jnp.broadcast_to(rows_done(2), (8, W))
     m = [jnp.broadcast_to(jnp.sum(jnp.where(lane == 8 * sub8 + k, summed, 0.0), axis=1, keepdims=True), (8, W)) for k in range(8)]
 
     def dot(p, q):
@@ -298,12 +311,11 @@
     for i in range(ITERS + 1):
         res_ref[i] = res[i]
 
-    for cp in basis_copies:
-        cp.wait()
     sn_copy.wait_send()
     for i in range(2):
         pair_copies[i].wait_send()
-        all_copy(i).wait_send()
+    for k, (into, group) in enumerate(((plane_in, PLANE), (line_in, LINE), (all_in, CUBE))):
+        row_all(into, k, len(group)).wait_send()
     for t in range(ITERS):
         if t != 1:
             halo_copies[t].wait_send()
@@ -321,7 +333,7 @@
         kernel,
         out_shape=(jax.ShapeDtypeStruct((ITERS + 1,) + vec, F32), coef, coef),
         in_specs=[anym] * 6,
-        out_specs=(anym, vmem, vmem),
+        out_specs=(vmem, vmem, vmem),
         scratch_shapes=[
             pltpu.SMEM((SLOTS, ROWS), jnp.int32),
             pltpu.SMEM((ROWS,), jnp.int32),
@@ -333,7 +345,6 @@
             pltpu.VMEM((8, W, 2 * W), BF16),
             pltpu.VMEM((2 * ROWS * NRHS, 512), BF16),
             pltpu.VMEM((64, 8, W), F32),
-            pltpu.VMEM((ITERS + 1,) + vec, F32),
             pltpu.VMEM((ITERS,) + vec, F32),
             pltpu.VMEM((ITERS,) + vec, F32),
             pltpu.VMEM((ITERS,) + vec, F32),
@@ -344,11 +355,12 @@
             pltpu.VMEM(vec, F32),
             pltpu.VMEM((2 * ROWS, 16, W), BF16),
             pltpu.VMEM((512, 2 * W), BF16),
-            pltpu.VMEM((4, 8, W), F32),
+            pltpu.VMEM((5, 8, W), F32),
             pltpu.VMEM((2, 8, W), F32),
-            pltpu.VMEM((2, SLABS - 1, 1, W), F32),
+            pltpu.VMEM((SLABS, W), F32),
+            pltpu.VMEM((16, W), F32),
+            pltpu.VMEM((8, W), F32),
             dma((5,)),
-            dma((ITERS + 1,)),
             dma((4,)),
             dma((ITERS,)),
             dma((ITERS,)),
@@ -360,11 +372,11 @@
             dma,
             dma((2,)),
             dma((2,)),
-            dma((2,)),
-            dma((2,)),
+            dma((3,)),
+            dma((3,)),
         ],
-        compiler_params=pltpu.CompilerParams(collective_id=0, has_side_effects=True, vmem_limit_bytes=60 << 20),
-    )(tile_cols.T, tile_counts, right_side, diagonal, dense_blocks, tiles)
+        compiler_params=pltpu.CompilerParams(collective_id=0, has_side_effects=True, vmem_limit_bytes=44 << 20),
+    )(*[pltpu.with_memory_space_constraint(a, pltpu.HBM) for a in (tile_cols.T, tile_counts, right_side, diagonal, dense_blocks, tiles)])
     x = jnp.sum(sol[:, None] * basis, axis=0)
     r = jnp.sum(res[:, None] * basis, axis=0)
     return x, r

time: 48.1 us -> 46.3 us (0.963)
  other arithmetic: 1.7 us -> 0.7 us
  Pallas kernels: 45.6 us -> 44.8 us
    reduce_sum x1, other arithmetic: 1.7 us -> 0.7 us  [body(): r = jnp.sum(res[:, None] * basis, axis=0)]
    pallas_call x1, Pallas kernels: 45.6 us -> 44.8 us  [body(): pl.pallas_call(kernel, out_shape=(jax.ShapeDtypeStruct((ITERS + 1,) + vec...]
where the time goes in v4:
time: 46.3 us; the launch traced here: 46.2 us
  Pallas kernels  44.8 us (97%)
  other arithmetic  0.7 us (2%)
  between operations  0.64 us (1%)
    pallas_call x1, Pallas kernels, body(): pl.pallas_call(kernel, out_shape=(jax.ShapeDtypeStruct((ITERS + 1,) + vec...  44.8 us

profile of v4, /device:TPU:0, one launch (start us, length us, event | category | flops | bytes accessed | tf_op | source)
XLA Modules:
  0.0 46.2 jit_solution(1742751247388734905)
XLA Ops:
  0.6 44.8 %shard_map.77 = (f32[5,16,8,128]{3,2,1,0:T(8,128)S(1)}, f32[5,8,128]{2,1,0:T(8,128)S(1)}, f32[5,8,128]{2,1,0:T(8,128)S(1)}) custom-call(s32[4,16]{1,0:T(4,128)} %bitcast.1, s32[16]{0:T(128)} %counts_hbm.1, f32[16,8,128]{2,1,0:T(8,128)} %b_hbm.1, f32[16,128]{1,0:T(8,128)} %diag_hbm.1, f32[8,128,128]{2,1,0:T(8,128)} %dense_hbm.1, f32[16,4,128,128]{3,2,1,0:T(8,128)} %tiles_hbm.1), custom_call_target="tpu_custom_call" | custom-call | tf_op jit(solution)/shard_map/pallas_call | solution.py:332
  45.5 0.7 %multiply_reduce_fusion = (f32[16,8,128]{2,1,0:T(8,128)}, f32[16,8,128]{2,1,0:T(8,128)}) fusion(f32[5,16,8,128]{3,2,1,0:T(8,128)S(1)} %get-tuple-element.6, f32[5,8,128]{2,1,0:T(8,128)S(1)} %get-tuple-element.7, f32[5,8,128]{2,1,0:T(8,128)S(1)} %get-tuple-element.5), kind=kLoop, calls=%fused_computation | loop fusion | flops 294912 | bytes 499712 | tf_op jit(solution)/shard_map/reduce_sum | solution.py:381

commit v5 on v4

--- a/solution.py
+++ b/solution.py
@@ -27,13 +27,13 @@
 
 
 CUBE = sorted([(a, b, d) for a in range(4) for b in range(4) for d in range(4) if (a, b, d) != (0, 0, 0)], key=far, reverse=True)
-PLANE = [o for o in CUBE if o[0] == 0]
-LINE = [o for o in CUBE if o[1] == 0 and o[2] == 0]
+AXES = [[tuple(d if i == a else 0 for i in range(3)) for d in (2, 1, 3)] for a in (2, 1, 0)]
+GROUPS = AXES + [CUBE]
 
 
 def kernel(cols_hbm, counts_hbm, b_hbm, diag_hbm, dense_hbm, tiles_hbm, krylov, sol_ref, res_ref,
            cols, counts, diag_ref, tf, df, wt, wf, dw, gm, sq, halo, qout, qin, pout, pin, dg, snout, snin, vs, bst,
-           pair_out, pair_in, all_in, plane_in, line_in, in_sem, tile_sem, peer_ss, peer_rs, halo_ss, halo_rs, q_ss, q_rs, sn_ss, sn_rs, pair_ss, pair_rs, row_ss, row_rs):
+           pair_out, pair_in, all_in, y_in, x_in, z_in, in_sem, tile_sem, peer_ss, peer_rs, halo_ss, halo_rs, q_ss, q_rs, sn_ss, sn_rs, pair_ss, pair_rs, row_ss, row_rs):
     s = lax.axis_index("slab")
     c = lax.axis_index("sub")
     after = ((s + 1) % SLABS, 1 - c)
@@ -48,8 +48,26 @@
         cp.start()
 
     barrier = pltpu.get_barrier_semaphore()
-    for dev in (peer, after, before):
-        pl.semaphore_signal(barrier, inc=1, device_id=dev, device_id_type=MESH)
+    has_after, has_before = s < SLABS - 1, s > 0
+
+    @pl.when(has_after)
+    def _():
+        pl.semaphore_signal(barrier, inc=1, device_id=after, device_id_type=MESH)
+
+    @pl.when(has_before)
+    def _():
+        pl.semaphore_signal(barrier, inc=1, device_id=before, device_id_type=MESH)
+
+    @pl.when(jnp.logical_not(has_before))
+    def _():
+        qin[...] = jnp.zeros_like(qin)
+        snin[...] = jnp.zeros_like(snin)
+
+    @pl.when(jnp.logical_not(has_after))
+    def _():
+        halo[...] = jnp.zeros_like(halo)
+
+    pl.semaphore_signal(barrier, inc=1, device_id=peer, device_id_type=MESH)
 
     z, xx, yy = s // 16, (s // 4) % 4, s % 4
 
@@ -57,7 +75,7 @@
         a, b, d = offset
         return (((z + a) % 4) * 16 + ((xx + b) % 4) * 4 + (yy + d) % 4, c)
 
-    for offset in CUBE:
+    for offset in AXES[0] + AXES[1] + AXES[2]:
         pl.semaphore_signal(barrier, inc=1, device_id=moved(offset), device_id_type=MESH)
 
     def remote(src, dst, ss, rs, dev):
@@ -119,7 +137,13 @@
                 sq[r * SLOTS + k] = jnp.sum((t * t).reshape(16, 8, W), axis=0)
             back(r)
     spread_q(0)
-    pl.semaphore_wait(barrier, SLABS + 2)
+    pl.semaphore_wait(barrier, 10 + has_after.astype(jnp.int32) + has_before.astype(jnp.int32))
+
+    def when_call(cond, call):
+        @pl.when(cond)
+        def _():
+            call()
+
 
     halo_copies = [remote(krylov.at[t], halo.at[t], halo_ss.at[t], halo_rs.at[t], before) for t in range(ITERS)]
     q_copies = [remote(qout.at[t], qin.at[t], q_ss.at[t], q_rs.at[t], after) for t in range(ITERS)]
@@ -127,6 +151,8 @@
     sn_copy = remote(snout, snin, sn_ss, sn_rs, after)
     pair_copies = [remote(pair_out.at[i], pair_in.at[i], pair_ss.at[i], pair_rs.at[i], peer) for i in range(2)]
 
+    lands = (y_in, x_in, z_in, all_in)
+
     def pair_sum(i):
         pair_copies[i].wait_recv()
         return pair_out[i, 0:1] + pair_in[i, 0:1]
@@ -139,17 +165,17 @@
 
     def rows_start(k, row):
         pair_out[2 + k, 0:1] = row
-        for cp in row_copies(pair_out.at[2 + k, pl.ds(0, 1)], (plane_in, line_in, all_in)[k], k, (PLANE, LINE, CUBE)[k]):
+        for cp in row_copies(pair_out.at[2 + k, pl.ds(0, 1)], lands[k], k, GROUPS[k]):
             cp.start()
 
     def rows_done(k):
-        into, count = ((plane_in, len(PLANE)), (line_in, len(LINE)), (all_in, len(CUBE)))[k]
+        into, count = lands[k], len(GROUPS[k])
         row_all(into, k, count).wait_recv()
         into[count:count + 1] = pair_out[2 + k, 0:1]
         return jnp.sum(into[0:count + 1], axis=0, keepdims=True)
 
-    halo_copies[0].start()
-    q_copies[0].start()
+    when_call(has_before, halo_copies[0].start)
+    when_call(has_after, q_copies[0].start)
 
     sigma = jnp.broadcast_to(jnp.sqrt(jnp.sum(jnp.sum(sq[...], axis=2, keepdims=True), axis=1, keepdims=True)), (64, 8, W))
     sigma2 = sigma.reshape(512, W)
@@ -161,7 +187,7 @@
     scol = scol[:, :W] + scol[:, W:] + jnp.dot(gm[...], s_lo, preferred_element_type=F32)
     scol = scol.reshape(2 * ROWS, NRHS, W)
     snout[...] = scol[ROWS:]
-    sn_copy.start()
+    when_call(has_after, sn_copy.start)
 
     small_copies[3].wait()
     small_copies[4].wait()
@@ -228,12 +254,12 @@
     theta = None
     for t in range(ITERS):
         if t > 0:
-            halo_copies[t].start()
+            when_call(has_before, halo_copies[t].start)
             own_parts(t)
             for r in range(ROWS):
                 back(r)
             spread_q(t)
-            q_copies[t].start()
+            when_call(has_after, q_copies[t].start)
         seen = local_part(t)
         if t == 2:
             for i, j in [(0, 0), (0, 1), (1, 1), (1, 2), (2, 2)]:
@@ -247,30 +273,32 @@
             rows_start(0, pair_sum(0))
             for r in range(8, ROWS):
                 wf[r] = wt[r].T
-        halo_copies[t].wait_recv()
+        if t == 1:
+            rows_start(2, rows_done(1))
+        when_call(has_after, halo_copies[t].wait_recv)
         crossed = forward(t)
         if t == 3:
             row = 0.5 * moments + place(7, seen + 2.0 * crossed, jnp.zeros((8, W), F32))
             pair_out[1] = jnp.broadcast_to(jnp.sum(row, axis=0, keepdims=True), (8, W))
             pair_copies[1].start()
         if t == 0:
-            sn_copy.wait_recv()
+            when_call(has_before, sn_copy.wait_recv)
             dg[...] = dg[...] + snin[...]
             pout[t] = pout[t] + snin[...] * krylov[t]
-        q_copies[t].wait_recv()
+        when_call(has_before, q_copies[t].wait_recv)
         pout[t] = pout[t] + qin[t]
         p_copies[t].start()
         if t == 3:
-            rows_start(2, pair_sum(1))
+            rows_start(3, pair_sum(1))
         if t == 0:
             rows_start(1, rows_done(0))
         if t == 1:
-            theta = jnp.broadcast_to(rows_done(1) * (1.0 / (SLABS * ROWS * W)), (8, W))
+            theta = jnp.broadcast_to(rows_done(2) * (1.0 / (SLABS * ROWS * W)), (8, W))
             dg[...] = dg[...] - 0.5 * theta
         p_copies[t].wait_recv()
         image = pout[t] + pin[t]
         if t == 1:
-            halo_copies[1].wait_send()
+            when_call(has_before, halo_copies[1].wait_send)
             plain = krylov[1]
             one = plain - theta * krylov[0]
             krylov[1] = one
@@ -278,7 +306,7 @@
         else:
             krylov[t + 1] = image
 
-    summed = jnp.broadcast_to(rows_done(2), (8, W))
+    summed = jnp.broadcast_to(rows_done(3), (8, W))
     m = [jnp.broadcast_to(jnp.sum(jnp.where(lane == 8 * sub8 + k, summed, 0.0), axis=1, keepdims=True), (8, W)) for k in range(8)]
 
     def dot(p, q):
@@ -311,15 +339,15 @@
     for i in range(ITERS + 1):
         res_ref[i] = res[i]
 
-    sn_copy.wait_send()
+    when_call(has_after, sn_copy.wait_send)
     for i in range(2):
         pair_copies[i].wait_send()
-    for k, (into, group) in enumerate(((plane_in, PLANE), (line_in, LINE), (all_in, CUBE))):
+    for k, (into, group) in enumerate(zip(lands, GROUPS)):
         row_all(into, k, len(group)).wait_send()
     for t in range(ITERS):
         if t != 1:
-            halo_copies[t].wait_send()
-        q_copies[t].wait_send()
+            when_call(has_before, halo_copies[t].wait_send)
+        when_call(has_after, q_copies[t].wait_send)
         p_copies[t].wait_send()
 
 
@@ -355,10 +383,11 @@
             pltpu.VMEM(vec, F32),
             pltpu.VMEM((2 * ROWS, 16, W), BF16),
             pltpu.VMEM((512, 2 * W), BF16),
-            pltpu.VMEM((5, 8, W), F32),
+            pltpu.VMEM((6, 8, W), F32),
             pltpu.VMEM((2, 8, W), F32),
             pltpu.VMEM((SLABS, W), F32),
-            pltpu.VMEM((16, W), F32),
+            pltpu.VMEM((8, W), F32),
+            pltpu.VMEM((8, W), F32),
             pltpu.VMEM((8, W), F32),
             dma((5,)),
             dma((4,)),
@@ -372,8 +401,8 @@
             dma,
             dma((2,)),
             dma((2,)),
-            dma((3,)),
-            dma((3,)),
+            dma((4,)),
+            dma((4,)),
         ],
         compiler_params=pltpu.CompilerParams(collective_id=0, has_side_effects=True, vmem_limit_bytes=44 << 20),
     )(*[pltpu.with_memory_space_constraint(a, pltpu.HBM) for a in (tile_cols.T, tile_counts, right_side, diagonal, dense_blocks, tiles)])

time: 46.3 us -> 43.3 us (0.935)
  Pallas kernels: 44.8 us -> 41.9 us
    pallas_call x1, Pallas kernels: 44.8 us -> 41.9 us  [body(): pl.pallas_call(kernel, out_shape=(jax.ShapeDtypeStruct((ITERS + 1,) + vec...]
where the time goes in v5:
time: 43.3 us; the launch traced here: 43.2 us
  Pallas kernels  41.9 us (97%)
  other arithmetic  0.7 us (2%)
  between operations  0.64 us (1%)
    pallas_call x1, Pallas kernels, body(): pl.pallas_call(kernel, out_shape=(jax.ShapeDtypeStruct((ITERS + 1,) + vec...  41.9 us

profile of v5, /device:TPU:0, one launch (start us, length us, event | category | flops | bytes accessed | tf_op | source)
XLA Modules:
  0.0 43.2 jit_solution(265822372767539875)
XLA Ops:
  0.6 41.9 %shard_map.77 = (f32[5,16,8,128]{3,2,1,0:T(8,128)S(1)}, f32[5,8,128]{2,1,0:T(8,128)S(1)}, f32[5,8,128]{2,1,0:T(8,128)S(1)}) custom-call(s32[4,16]{1,0:T(4,128)} %bitcast.1, s32[16]{0:T(128)} %counts_hbm.1, f32[16,8,128]{2,1,0:T(8,128)} %b_hbm.1, f32[16,128]{1,0:T(8,128)} %diag_hbm.1, f32[8,128,128]{2,1,0:T(8,128)} %dense_hbm.1, f32[16,4,128,128]{3,2,1,0:T(8,128)} %tiles_hbm.1), custom_call_target="tpu_custom_call" | custom-call | tf_op jit(solution)/shard_map/pallas_call | solution.py:360
  42.5 0.7 %multiply_reduce_fusion = (f32[16,8,128]{2,1,0:T(8,128)}, f32[16,8,128]{2,1,0:T(8,128)}) fusion(f32[5,16,8,128]{3,2,1,0:T(8,128)S(1)} %get-tuple-element.6, f32[5,8,128]{2,1,0:T(8,128)S(1)} %get-tuple-element.7, f32[5,8,128]{2,1,0:T(8,128)S(1)} %get-tuple-element.5), kind=kLoop, calls=%fused_computation | loop fusion | flops 294912 | bytes 499712 | tf_op jit(solution)/shard_map/reduce_sum | solution.py:410

commit v6 on v5

--- a/solution.py
+++ b/solution.py
@@ -119,10 +119,14 @@
             bst[at:at + 16, 0:W] = hi
             bst[at:at + 16, W:2 * W] = lo
 
-    def spread_q(t):
-        spread = jnp.dot(gm[...], bst[...], preferred_element_type=F32)
-        spread = (spread[:, :W] + spread[:, W:]).reshape(2 * ROWS, NRHS, W)
-        qout[t] = spread[ROWS:]
+    def spread_high(t):
+        spread = jnp.dot(gm[192:256, 256:512], bst[256:512, :], preferred_element_type=F32)
+        qout[t, 8:ROWS] = (spread[:, :W] + spread[:, W:]).reshape(8, NRHS, W)
+
+    def spread_low(t):
+        spread = jnp.dot(gm[0:192, :], bst[...], preferred_element_type=F32)
+        spread = (spread[:, :W] + spread[:, W:]).reshape(24, NRHS, W)
+        qout[t, 0:8] = spread[ROWS:]
         pout[t] = spread[:ROWS]
 
     for i in range(4):
@@ -136,7 +140,8 @@
                 wt[r, W:2 * W, W * k:W * k + W] = lo
                 sq[r * SLOTS + k] = jnp.sum((t * t).reshape(16, 8, W), axis=0)
             back(r)
-    spread_q(0)
+    spread_high(0)
+    spread_low(0)
     pl.semaphore_wait(barrier, 10 + has_after.astype(jnp.int32) + has_before.astype(jnp.int32))
 
     def when_call(cond, call):
@@ -145,9 +150,12 @@
             call()
 
 
-    halo_copies = [remote(krylov.at[t], halo.at[t], halo_ss.at[t], halo_rs.at[t], before) for t in range(ITERS)]
-    q_copies = [remote(qout.at[t], qin.at[t], q_ss.at[t], q_rs.at[t], after) for t in range(ITERS)]
-    p_copies = [remote(pout.at[t], pin.at[t], peer_ss.at[t], peer_rs.at[t], peer) for t in range(ITERS)]
+    def halves(src, into, ss, rs, dev):
+        return [[remote(src.at[t, pl.ds(8 * h, 8)], into.at[t, pl.ds(8 * h, 8)], ss.at[t, h], rs.at[t, h], dev) for h in range(2)] for t in range(ITERS)]
+
+    halo_copies = halves(krylov, halo, halo_ss, halo_rs, before)
+    q_copies = halves(qout, qin, q_ss, q_rs, after)
+    p_copies = halves(pout, pin, peer_ss, peer_rs, peer)
     sn_copy = remote(snout, snin, sn_ss, sn_rs, after)
     pair_copies = [remote(pair_out.at[i], pair_in.at[i], pair_ss.at[i], pair_rs.at[i], peer) for i in range(2)]
 
@@ -174,8 +182,10 @@
         into[count:count + 1] = pair_out[2 + k, 0:1]
         return jnp.sum(into[0:count + 1], axis=0, keepdims=True)
 
-    when_call(has_before, halo_copies[0].start)
-    when_call(has_after, q_copies[0].start)
+    for h in range(2):
+        when_call(has_before, halo_copies[0][h].start)
+    for h in (1, 0):
+        when_call(has_after, q_copies[0][h].start)
 
     sigma = jnp.broadcast_to(jnp.sqrt(jnp.sum(jnp.sum(sq[...], axis=2, keepdims=True), axis=1, keepdims=True)), (64, 8, W))
     sigma2 = sigma.reshape(512, W)
@@ -236,13 +246,13 @@
             seen = seen + out * krylov[t, 8 * c + j]
         return seen
 
-    def forward(t):
-        for j in range(ROWS):
+    def forward(t, h):
+        for j in range(8 * h, 8 * h + 8):
             hi, lo = split(halo[t, j])
             vs[ROWS + j] = jnp.concatenate([hi.astype(F32), lo.astype(F32)], axis=0).astype(BF16)
         seen = jnp.zeros((8, W), F32)
-        for r in range(ROWS):
-            x = jnp.concatenate([vs[jnp.clip(cols[k, r] - first, 0, 2 * ROWS - 1)] for k in range(SLOTS)], axis=1)
+        for r in range(8 * h, 8 * h + 8):
+            x = jnp.concatenate([vs[jnp.clip(cols[k, r] - first, 0, ROWS + 8 * h + 7)] for k in range(SLOTS)], axis=1)
             out = jnp.dot(x, wf[r], preferred_element_type=F32)
             out = out[0:8] + out[8:16]
             out = out[:, :W] + out[:, W:]
@@ -254,12 +264,17 @@
     theta = None
     for t in range(ITERS):
         if t > 0:
-            when_call(has_before, halo_copies[t].start)
+            for h in range(2):
+                when_call(has_before, halo_copies[t][h].start)
             own_parts(t)
-            for r in range(ROWS):
+            for r in range(8, ROWS):
                 back(r)
-            spread_q(t)
-            when_call(has_after, q_copies[t].start)
+            spread_high(t)
+            when_call(has_after, q_copies[t][1].start)
+            for r in range(8):
+                back(r)
+            spread_low(t)
+            when_call(has_after, q_copies[t][0].start)
         seen = local_part(t)
         if t == 2:
             for i, j in [(0, 0), (0, 1), (1, 1), (1, 2), (2, 2)]:
@@ -275,30 +290,34 @@
                 wf[r] = wt[r].T
         if t == 1:
             rows_start(2, rows_done(1))
-        when_call(has_after, halo_copies[t].wait_recv)
-        crossed = forward(t)
+        crossed = seen * 0.5
+        for h in range(2):
+            when_call(has_after, halo_copies[t][h].wait_recv)
+            crossed = crossed + forward(t, h)
         if t == 3:
-            row = 0.5 * moments + place(7, seen + 2.0 * crossed, jnp.zeros((8, W), F32))
+            row = 0.5 * moments + place(7, 2.0 * crossed, jnp.zeros((8, W), F32))
             pair_out[1] = jnp.broadcast_to(jnp.sum(row, axis=0, keepdims=True), (8, W))
             pair_copies[1].start()
+            rows_start(3, pair_sum(1))
         if t == 0:
             when_call(has_before, sn_copy.wait_recv)
             dg[...] = dg[...] + snin[...]
             pout[t] = pout[t] + snin[...] * krylov[t]
-        when_call(has_before, q_copies[t].wait_recv)
-        pout[t] = pout[t] + qin[t]
-        p_copies[t].start()
-        if t == 3:
-            rows_start(3, pair_sum(1))
+        for h in (1, 0):
+            when_call(has_before, q_copies[t][h].wait_recv)
+            pout[t, 8 * h:8 * h + 8] = pout[t, 8 * h:8 * h + 8] + qin[t, 8 * h:8 * h + 8]
+            p_copies[t][h].start()
         if t == 0:
             rows_start(1, rows_done(0))
         if t == 1:
             theta = jnp.broadcast_to(rows_done(2) * (1.0 / (SLABS * ROWS * W)), (8, W))
             dg[...] = dg[...] - 0.5 * theta
-        p_copies[t].wait_recv()
+        p_copies[t][1].wait_recv()
+        p_copies[t][0].wait_recv()
         image = pout[t] + pin[t]
         if t == 1:
-            when_call(has_before, halo_copies[1].wait_send)
+            for h in range(2):
+                when_call(has_before, halo_copies[1][h].wait_send)
             plain = krylov[1]
             one = plain - theta * krylov[0]
             krylov[1] = one
@@ -345,10 +364,11 @@
     for k, (into, group) in enumerate(zip(lands, GROUPS)):
         row_all(into, k, len(group)).wait_send()
     for t in range(ITERS):
-        if t != 1:
-            when_call(has_before, halo_copies[t].wait_send)
-        when_call(has_after, q_copies[t].wait_send)
-        p_copies[t].wait_send()
+        for h in range(2):
+            if t != 1:
+                when_call(has_before, halo_copies[t][h].wait_send)
+            when_call(has_after, q_copies[t][h].wait_send)
+            p_copies[t][h].wait_send()
 
 
 def body(right_side, diagonal, dense_blocks, tiles, tile_cols, tile_counts):
@@ -391,12 +411,12 @@
             pltpu.VMEM((8, W), F32),
             dma((5,)),
             dma((4,)),
-            dma((ITERS,)),
-            dma((ITERS,)),
-            dma((ITERS,)),
-            dma((ITERS,)),
-            dma((ITERS,)),
-            dma((ITERS,)),
+            dma((ITERS, 2)),
+            dma((ITERS, 2)),
+            dma((ITERS, 2)),
+            dma((ITERS, 2)),
+            dma((ITERS, 2)),
+            dma((ITERS, 2)),
             dma,
             dma,
             dma((2,)),

time: 43.3 us -> 43.1 us (level)
  no operation moved by 1% of the time
where the time goes in v6:
time: 43.1 us; the launch traced here: 43 us
  Pallas kernels  41.7 us (97%)
  other arithmetic  0.7 us (2%)
  between operations  0.64 us (1%)
    pallas_call x1, Pallas kernels, body(): pl.pallas_call(kernel, out_shape=(jax.ShapeDtypeStruct((ITERS + 1,) + vec...  41.7 us

profile of v6, /device:TPU:0, one launch (start us, length us, event | category | flops | bytes accessed | tf_op | source)
XLA Modules:
  0.0 43.0 jit_solution(12668704901826430996)
XLA Ops:
  0.6 41.7 %shard_map.77 = (f32[5,16,8,128]{3,2,1,0:T(8,128)S(1)}, f32[5,8,128]{2,1,0:T(8,128)S(1)}, f32[5,8,128]{2,1,0:T(8,128)S(1)}) custom-call(s32[4,16]{1,0:T(4,128)} %bitcast.1, s32[16]{0:T(128)} %counts_hbm.1, f32[16,8,128]{2,1,0:T(8,128)} %b_hbm.1, f32[16,128]{1,0:T(8,128)} %diag_hbm.1, f32[8,128,128]{2,1,0:T(8,128)} %dense_hbm.1, f32[16,4,128,128]{3,2,1,0:T(8,128)} %tiles_hbm.1), custom_call_target="tpu_custom_call" | custom-call | tf_op jit(solution)/shard_map/pallas_call | solution.py:380
  42.3 0.7 %multiply_reduce_fusion = (f32[16,8,128]{2,1,0:T(8,128)}, f32[16,8,128]{2,1,0:T(8,128)}) fusion(f32[5,16,8,128]{3,2,1,0:T(8,128)S(1)} %get-tuple-element.6, f32[5,8,128]{2,1,0:T(8,128)S(1)} %get-tuple-element.7, f32[5,8,128]{2,1,0:T(8,128)S(1)} %get-tuple-element.5), kind=kLoop, calls=%fused_computation | loop fusion | flops 294912 | bytes 499712 | tf_op jit(solution)/shard_map/reduce_sum | solution.py:430
